TPU v7x, 512 devices: a whole 4x8x8 slice. The times are simulated.
512 devices in a mesh: row: 16 (over z, x_hi), col: 32 (over y, x_lo, core).
Axes of the slice: x: 4 (x_hi: 2, x_lo: 2; x = x_hi * 2 + x_lo), y: 8, z: 8, core: 2. Of those that a mesh axis runs over, the one named last changes fastest.
Arguments:
- matrix: float32 [16384, 16384], P('row', 'col'), as said below
- moves: int32 [1, 64], replicated, may hold values from 0 to 63, as said below
Outputs:
- result: float32 [16384, 16384], P('row', 'col')
Inputs may be any that keep to these rules, and one draw needn't show every extreme that they name: matrix is symmetric. Each moves[t] is a permutation of the 64 slots made of two rounds of swaps: first of some pairs of slots (2k+1, 2k+2), then of some pairs (2k, 2k+1).
All inputs are finite; a program needn't handle non-finite values.
Results may differ from a plain program's by a relative error of at most 0.0001.
Values sent between devices are 32-bit elements; how exact they have to be, the bound alone decides.
No kernel may reach another device: no remote copies, remote signals or barrier semaphores. Data moves between devices by JAX's collectives and lax.ppermute only.
A program may use at most 64 MiB of HBM per device.

v0:
```python
import math

import jax
import jax.numpy as jnp
from jax import lax
from jax.sharding import PartitionSpec as P

BLOCK = 256
NEWTON = 3


def from_root(x, axis, root):
    mine = lax.axis_index(axis) == root
    return lax.psum(jnp.where(mine, x, jnp.zeros_like(x)), axis)


def padded(block, sides, width):
    for axis, dim in sides:
        count = lax.axis_size(axis)
        forward = [(i, i + 1) for i in range(count - 1)]
        backward = [(target, source) for source, target in forward]
        low = lax.ppermute(
            lax.slice_in_dim(block, block.shape[dim] - width, None, axis=dim), axis, forward
        )
        high = lax.ppermute(lax.slice_in_dim(block, 0, width, axis=dim), axis, backward)
        block = jnp.concatenate([low, block, high], axis=dim)
    return block


def newton_step(root, gram):
    highest = lax.Precision.HIGHEST
    inner = jnp.dot(gram, root, precision=highest)
    inner = jnp.dot(root, inner, precision=highest)
    inner = jnp.dot(root, inner, precision=highest)
    return 1.5 * root - 0.5 * inner


def make_factors(upper):
    highest = lax.Precision.HIGHEST
    width = upper.shape[0]
    identity = jnp.eye(width, dtype=jnp.float32)
    coupling = upper * lax.rsqrt(jnp.sum(upper * upper) / width + 1e-06)
    left_gram = identity + jnp.dot(coupling, coupling.T, precision=highest)
    right_gram = identity + jnp.dot(coupling.T, coupling, precision=highest)
    left_root = identity * (1.0 / math.sqrt(5.0))
    right_root = left_root
    for sweep in range(NEWTON):
        left_root = newton_step(left_root, left_gram)
        right_root = newton_step(right_root, right_gram)
    return (left_root, right_root, coupling)


def assemble(left_root, right_root, coupling):
    highest = lax.Precision.HIGHEST
    top = jnp.concatenate([left_root, -jnp.dot(coupling, right_root, precision=highest)], axis=1)
    bottom = jnp.concatenate(
        [jnp.dot(coupling.T, left_root, precision=highest), right_root], axis=1
    )
    return jnp.concatenate([top, bottom], axis=0)


def build_payload(upper):
    left_root, right_root, coupling = make_factors(upper)
    return assemble(left_root, right_root, coupling)


def blank_payload(upper):
    width = upper.shape[0]
    return jnp.zeros((2 * width, 2 * width), jnp.float32)


def receive_down(payload, owner):
    return from_root(payload, "row", owner)


def receive_across(payload, owner):
    return from_root(payload, "col", owner)


def turn_rows(current, turns, block):
    highest = lax.Precision.HIGHEST
    pieces = []
    for member in range(len(turns)):
        band = current[2 * member * block : (2 * member + 2) * block]
        pieces.append(jnp.dot(turns[member].T, band, precision=highest))
    return jnp.concatenate(pieces, axis=0)


def turn_columns(current, turns):
    highest = lax.Precision.HIGHEST
    pieces = jnp.dot(current, turns[0], precision=highest)
    return pieces


def source_slots(order):
    count = order.shape[0]
    slots = jnp.arange(count, dtype=jnp.int32)
    hits = order[None, :] == slots[:, None]
    return jnp.sum(jnp.where(hits, slots[None, :], 0), axis=1)


def pick_blocks(extended, sources, first, here, block, axis_number):
    wanted = lax.dynamic_slice_in_dim(sources, first, here) - first + 1
    if axis_number == 0:
        grouped = extended.reshape(here + 2, block, extended.shape[1])
        return jnp.take(grouped, wanted, axis=0).reshape(here * block, extended.shape[1])
    grouped = extended.reshape(extended.shape[0], here + 2, block)
    return jnp.take(grouped, wanted, axis=1).reshape(extended.shape[0], here * block)


def body(matrix, moves):
    block = BLOCK
    row_here = matrix.shape[0] // block
    col_here = matrix.shape[1] // block
    row_pairs = row_here // 2
    col_pairs = col_here // 2
    row_index = lax.axis_index("row")
    col_index = lax.axis_index("col")
    current = matrix
    member = 0
    pair = col_index * col_pairs + member
    owner = 2 * pair // row_here
    offset = jnp.clip(2 * pair - row_index * row_here, 0, row_here - 2)
    upper = lax.dynamic_slice(current, (offset * block, (2 * member + 1) * block), (block, block))
    made = [lax.cond(owner == row_index, build_payload, blank_payload, upper)]
    member = 0
    owner = 2 * (col_index * col_pairs + member) // row_here
    column_turns = [receive_down(made[member], owner)]
    stacked = jnp.stack(made)
    row_turns = []
    for member in range(row_pairs):
        pair = row_index * row_pairs + member
        owner = 2 * pair // col_here
        chosen = jnp.clip(pair - col_index * col_pairs, 0, col_pairs - 1)
        row_turns.append(receive_across(stacked[chosen], owner))
    current = turn_columns(turn_rows(current, row_turns, block), column_turns)
    sources = source_slots(moves[0])
    row_first = row_index * row_here
    col_first = col_index * col_here
    extended = padded(current, (("row", 0),), block)
    current = pick_blocks(extended, sources, row_first, row_here, block, 0)
    extended = padded(current, (("col", 1),), block)
    current = pick_blocks(extended, sources, col_first, col_here, block, 1)
    return current


def solution(mesh):
    placed = (P("row", "col"), P())
    return jax.shard_map(
        body, mesh=mesh, in_specs=placed, out_specs=P("row", "col"), check_vma=False
    )
```

profile of v0, /device:TPU:37, one launch (start us, length us, event | category | flops | bytes accessed | tf_op | source)
XLA Modules:
  0.0 522.1 jit_solution(9806572094591967887)
XLA Ops:
  6.5 0.0 all-reduce.6.cloned.1.call-start
  6.5 0.1 conditional.1
  6.5 0.1 broadcast.53
  6.7 1.8 broadcast_select_fusion.3
  8.5 0.0 copy-start
  8.5 0.0 all-reduce.6.cloned.1.call-update
  8.5 0.2 all-reduce.4.cloned.1.call-start
  8.7 0.5 all-reduce.4.cloned.1.call-update
  9.2 252.1 %all-reduce.6.cloned.1.call-done = (f32[512,512]{1,0:T(8,128)}, f32[512,512]{1,0:T(8,128)}) async-done(((f32[512,512]{1,0:T(8,128)}, f32[512,512]{1,0:T(8,128)}), (f32[512,512]{1,0:T(8,128)}, f32[512,512]{1,0:T(8,128)})) %all-reduce.6.cloned.1.call-update) | async-done | bytes 2097168 | tf_op jit(solution)/shard_map/psum | solution.py:14
  261.3 0.0 copy-start.1
  261.3 0.0 copy-done
  261.3 3.2 fusion.53
  264.5 0.0 copy-done.1
  264.5 2.8 fusion.55
  267.3 156.8 %all-reduce.4.cloned.1.call-done = f32[512,512]{1,0:T(8,128)} async-done(((f32[512,512]{1,0:T(8,128)}), f32[512,512]{1,0:T(8,128)}) %all-reduce.4.cloned.1.call-update) | async-done | bytes 1048592 | tf_op jit(solution)/shard_map/psum | solution.py:14
  424.1 5.0 fusion.49
  429.1 0.0 copy-start.2
  429.1 1.0 fusion.59
  430.1 2.0 collective-permute-start
  432.1 4.8 collective-permute-start.1
  436.9 0.0 copy-done.2
  436.9 0.1 select_reduce_fusion
  437.0 0.1 compare_and_fusion
  437.1 0.1 broadcast_in_dim.49
  437.2 10.7 %collective-permute-done = f32[256,512]{1,0:T(8,128)S(1)} collective-permute-done((f32[256,512]{1,0:T(8,128)}, f32[256,512]{1,0:T(8,128)S(1)}, u32[]{:S(2)}, u32[]{:S(2)}) %collective-permute-start) | collective-permute-done | bytes 524320 | tf_op jit(solution)/shard_map/ppermute | solution.py:22
  447.9 0.0 collective-permute-done.1
  447.9 1.9 pad_maximum_fusion.1
  449.9 2.6 gather_fusion
  452.5 1.8 copy.51
  454.3 1.8 broadcast_select_fusion
  456.0 1.2 fusion.58
  457.2 13.9 %collective-permute-start.2 = (f32[1024,256]{0,1:T(8,128)}, f32[1024,256]{0,1:T(8,128)}, u32[]{:S(2)}, u32[]{:S(2)}) collective-permute-start(f32[1024,256]{0,1:T(8,128)} %get-tuple-element.59), channel_id=1, source_target_pairs={{0,1},{1,2},{2,3},{3,4},{4,5},{5,6},{6,7},{7,8},{8,9},{9,10},{10,1... | collective-permute-start | bytes 3145736 | tf_op jit(solution)/shard_map/ppermute | solution.py:22
  471.2 1.9 collective-permute-start.3
  473.1 0.1 compare_and_fusion.1
  473.2 0.1 broadcast_in_dim.46
  473.3 21.2 %collective-permute-done.2 = f32[1024,256]{0,1:T(8,128)} collective-permute-done((f32[1024,256]{0,1:T(8,128)}, f32[1024,256]{0,1:T(8,128)}, u32[]{:S(2)}, u32[]{:S(2)}) %collective-permute-start.2) | collective-permute-done | bytes 1048608 | tf_op jit(solution)/shard_map/ppermute | solution.py:22
  494.4 3.2 collective-permute-done.3
  497.6 4.0 pad_maximum_fusion
  501.6 5.4 %copy.40 = f32[1024,4,256]{2,0,1:T(8,128)} copy(f32[1024,4,256]{0,2,1:T(8,128)} %bitcast.42) | data formatting | bytes 8388608 | tf_op jit(solution)/shard_map/reshape | solution.py:107
  507.0 2.9 gather_fusion.1
  509.9 1.8 copy.41
  511.7 1.8 bitcast_select_fusion
  513.5 1.8 copy.42
  (4 shorter events, 0.0 us)
Async XLA Ops:
  6.5 254.8 %all-reduce.6.cloned.1.call-start = ((), (), s32[]{:S(2)}) async-start(), calls=%async_computation.1 | async-start | bytes 4194304 | tf_op jit(solution)/shard_map/psum | solution.py:14
  8.5 252.8 %copy-start = (f32[1024,512]{1,0:T(8,128)S(1)}, f32[1024,512]{1,0:T(8,128)}, u32[]{:S(2)}) copy-start(f32[1024,512]{1,0:T(8,128)} %param.4) | copy-start | bytes 6291460
  8.5 415.6 %all-reduce.4.cloned.1.call-start = ((), (), s32[]{:S(2)}) async-start(), calls=%async_computation | async-start | bytes 2097152 | tf_op jit(solution)/shard_map/psum | solution.py:14
  261.3 3.2 copy-start.1
  429.1 7.9 %copy-start.2 = (s32[1,64]{1,0:T(1,128)S(1)}, s32[1,64]{1,0:T(1,128)}, u32[]{:S(2)}) copy-start(s32[1,64]{1,0:T(1,128)} %param.5) | copy-start | bytes 772
  430.1 17.8 %collective-permute-start = (f32[256,512]{1,0:T(8,128)}, f32[256,512]{1,0:T(8,128)S(1)}, u32[]{:S(2)}, u32[]{:S(2)}) collective-permute-start(f32[256,512]{1,0:T(8,128)} %get-tuple-element.61), channel_id=1, source_target_pairs={{0,32},{32,64},{64,96},{96,128},{128,160},{160,192},{192,224},{224... | collective-permute-start | bytes 1572872 | tf_op jit(solution)/shard_map/ppermute | solution.py:22
  432.1 15.8 %collective-permute-start.1 = (f32[256,512]{1,0:T(8,128)}, f32[256,512]{1,0:T(8,128)S(1)}, u32[]{:S(2)}, u32[]{:S(2)}) collective-permute-start(f32[256,512]{1,0:T(8,128)} %get-tuple-element.62), channel_id=1, source_target_pairs={{32,0},{64,32},{96,64},{128,96},{160,128},{192,160},{224,192},{256... | collective-permute-start | bytes 1572872 | tf_op jit(solution)/shard_map/ppermute | solution.py:25
  457.2 37.2 %collective-permute-start.2 = (f32[1024,256]{0,1:T(8,128)}, f32[1024,256]{0,1:T(8,128)}, u32[]{:S(2)}, u32[]{:S(2)}) collective-permute-start(f32[1024,256]{0,1:T(8,128)} %get-tuple-element.59), channel_id=1, source_target_pairs={{0,1},{1,2},{2,3},{3,4},{4,5},{5,6},{6,7},{7,8},{8,9},{9,10},{10,1... | collective-permute-start | bytes 3145736 | tf_op jit(solution)/shard_map/ppermute | solution.py:22
  471.2 26.5 %collective-permute-start.3 = (f32[1024,256]{0,1:T(8,128)S(1)}, f32[1024,256]{0,1:T(8,128)}, u32[]{:S(2)}, u32[]{:S(2)}) collective-permute-start(f32[1024,256]{0,1:T(8,128)S(1)} %get-tuple-element.60), channel_id=1, source_target_pairs={{1,0},{2,1},{3,2},{4,3},{5,4},{6,5},{7,6},{8,7},{9,8},{10,9},{11,1... | collective-permute-start | bytes 3145736 | tf_op jit(solution)/shard_map/ppermute | solution.py:25
Sparse Core Ops, SparseCore 0:
  10.3 250.9 all-reduce.5
  264.5 159.5 all-reduce.3
where the time goes:
time: 523 us; the launch traced here: 522 us
  waiting for transfers between devices  444 us (85%)
  starting transfers between devices  22.9 us (4%)
  local copies, waits for them, and re-layouts  18.8 us (4%)
  between operations  13.5 us (3%)
  other arithmetic  11.6 us (2%)
  matrix products  11 us (2%)
    psum x2, waiting for transfers between devices, from_root(): return lax.psum(jnp.where(mine, x, jnp.zeros_like(x)), axis)  409 us
    ppermute x2, waiting for transfers between devices, padded(): lax.ppermute(lax.slice_in_dim(block, block.shape[dim] - width, None, axis...  31.9 us
    ppermute x2, starting transfers between devices, padded(): lax.ppermute(lax.slice_in_dim(block, block.shape[dim] - width, None, axis...  15.9 us
  transfers between devices with their start and end apart: 6, of which 5 were waited for; matrix products, arithmetic and copies ran while one was open for 1% of the time, Pallas kernels for 0%

commit v1 on v0

v1 whole, which is shorter than its diff:
```python
import functools
import math

import jax
import jax.numpy as jnp
from jax import lax
from jax.experimental import pallas as pl
from jax.experimental.pallas import tpu as pltpu
from jax.sharding import PartitionSpec as P

BLOCK = 256
SPAN = 2 * BLOCK
AXES = ("row", "col")
VMEM_LIMIT = 32 * 1024 * 1024


def split(x):
    high = x.astype(jnp.bfloat16)
    low = (x - high.astype(jnp.float32)).astype(jnp.bfloat16)
    return high, low


def mul(a, b):
    dot = functools.partial(jnp.dot, preferred_element_type=jnp.float32)
    return dot(a[0], b[0]) + (dot(a[0], b[1]) + dot(a[1], b[0]))


def identity():
    rows = lax.broadcasted_iota(jnp.int32, (BLOCK, BLOCK), 0)
    columns = lax.broadcasted_iota(jnp.int32, (BLOCK, BLOCK), 1)
    return jnp.where(rows == columns, 1.0, 0.0).astype(jnp.float32)


def factors(uppers):
    eye = identity()
    first = 1.0 / math.sqrt(5.0)
    alpha, beta = 1.5 * first, -0.5 * first**3
    couplings, grams = [], []
    for upper in uppers:
        total = jnp.sum(jnp.sum(upper * upper, axis=1, keepdims=True), axis=0, keepdims=True)
        coupling = upper * lax.rsqrt(total / BLOCK + 1e-06)
        here, turned = split(coupling), split(coupling.T)
        couplings.append(here)
        grams.append(eye + mul(here, turned))
        grams.append(eye + mul(turned, here))
    parts = [split(gram) for gram in grams]
    squares = [mul(part, part) for part in parts]
    square_parts = [split(square) for square in squares]
    inner = [
        split(1.5 * alpha * beta**2 * gram + 0.5 * beta**3 * square) for gram, square in zip(grams, squares)
    ]
    seconds = [
        1.5 * alpha * eye + (1.5 * beta - 0.5 * alpha**3) * gram - 1.5 * alpha**2 * beta * square - mul(part, rest)
        for gram, square, part, rest in zip(grams, squares, square_parts, inner)
    ]
    second_parts = [split(second) for second in seconds]
    twice = [split(mul(part, part)) for part in second_parts]
    scaled = [split(mul(gram, part)) for gram, part in zip(parts, second_parts)]
    roots = [1.5 * second - 0.5 * mul(a, b) for second, a, b in zip(seconds, twice, scaled)]
    results = []
    for number, coupling in enumerate(couplings):
        left, right = roots[2 * number], roots[2 * number + 1]
        cross = mul(split(left), coupling)
        results.append((left, cross, cross.T, right))
    return results


def columns_kernel(parity, matrix, token, away, near, held, turned, loaded, stored):
    rows = matrix.shape[0]
    chunk = BLOCK
    loads = [
        pltpu.make_async_copy(matrix.at[pl.ds(k * chunk, chunk)], held.at[pl.ds(k * chunk, chunk)], loaded.at[k])
        for k in range(rows // chunk)
    ]
    for load in loads:
        load.start()
    left, cross, crossed, right = factors([token[...]])[0]
    even = parity[0] == 0
    first = jnp.concatenate([left, crossed], axis=0)
    second = jnp.concatenate([-cross, right], axis=0)
    turn = split(jnp.concatenate([jnp.where(even, first, second), jnp.where(even, second, first)], axis=1))
    stores = []
    for k in range(rows // chunk):
        here = pl.ds(k * chunk, chunk)
        loads[k].wait()
        turned[here, :] = mul(split(held[here, :]), turn)
        for half, target in enumerate((away, near)):
            store = pltpu.make_async_copy(
                turned.at[here, pl.ds(half * BLOCK, BLOCK)], target.at[here], stored.at[2 * k + half]
            )
            store.start()
            stores.append(store)
    for store in stores:
        store.wait()


def rotations_kernel(parity, mine, other, high, low):
    even = parity[0] == 0
    uppers = [jnp.where(even, mine[...], other[...]), jnp.where(even, other[...], mine[...])]
    for member, (left, cross, crossed, right) in enumerate(factors(uppers)):
        parts = split(
            jnp.concatenate(
                [jnp.concatenate([left, cross], axis=1), jnp.concatenate([-crossed, right], axis=1)], axis=0
            )
        )
        high[member], low[member] = parts


def gather_columns(chosen, sources, held, sems, pair, start):
    rows = pl.ds(pair * SPAN, SPAN)
    for half in range(2):
        for number, source in enumerate(sources):

            @pl.when(chosen[half] == number)
            def _():
                copy = pltpu.make_async_copy(
                    source.at[rows], held.at[rows, pl.ds(half * BLOCK, BLOCK)], sems.at[2 * pair + half]
                )
                copy.start() if start else copy.wait()


def edge_rows_kernel(chosen, s0, s1, s2, s3, high, low, send_a, send_b, held, edge, loaded, stored):
    sources = (s0, s1, s2, s3)
    for pair in range(2):
        gather_columns(chosen, sources, held, loaded, pair, True)
    for pair in range(2):
        gather_columns(chosen, sources, held, loaded, pair, False)
        lines = pl.ds(pair * BLOCK, BLOCK)
        edge[pair] = mul((high[pair, lines], low[pair, lines]), split(held[pl.ds(pair * SPAN, SPAN), :]))
        for even, target in ((pair == 1, send_a), (pair == 0, send_b)):

            @pl.when((chosen[2] == 0) == even)
            def _():
                pltpu.make_async_copy(edge.at[pair], target, stored.at[pair]).start()

    for pair in range(2):
        pltpu.make_async_copy(edge.at[pair], send_a, stored.at[pair]).wait()


def inner_rows_kernel(
    chosen, place, s0, s1, s2, s3, high, low, send_a, send_b, result, held, inside, loaded, stored
):
    sources = (s0, s1, s2, s3)
    for pair in range(2):
        gather_columns(chosen, sources, held, loaded, pair, True)
    for slot, source in ((0, send_b), (3, send_a)):
        for even, edge in ((True, source), (False, send_a if slot == 0 else send_b)):

            @pl.when((place[slot] >= 0) & ((chosen[2] == 0) == even))
            def _():
                spot = pl.multiple_of(place[slot] * BLOCK, BLOCK)
                pltpu.make_async_copy(edge, result.at[pl.ds(spot, BLOCK)], stored.at[slot]).start()

    for pair in range(2):
        gather_columns(chosen, sources, held, loaded, pair, False)
        lines = pl.ds((1 - pair) * BLOCK, BLOCK)
        inside[pair] = mul((high[pair, lines], low[pair, lines]), split(held[pl.ds(pair * SPAN, SPAN), :]))
        spot = pl.multiple_of(place[1 + pair] * BLOCK, BLOCK)
        pltpu.make_async_copy(inside.at[pair], result.at[pl.ds(spot, BLOCK)], stored.at[1 + pair]).start()
    for slot in range(4):

        @pl.when(place[slot] >= 0)
        def _():
            pltpu.make_async_copy(inside.at[0], result.at[pl.ds(0, BLOCK)], stored.at[slot]).wait()


def arrivals_kernel(place, got_a, got_b, partial, result, stored):
    del partial
    for number, got in enumerate((got_a, got_b)):

        @pl.when(place[number] >= 0)
        def _():
            spot = pl.multiple_of(place[number] * BLOCK, BLOCK)
            pltpu.make_async_copy(got, result.at[pl.ds(spot, BLOCK)], stored.at[number]).start()

    for number, got in enumerate((got_a, got_b)):

        @pl.when(place[number] >= 0)
        def _():
            pltpu.make_async_copy(got, result.at[pl.ds(0, BLOCK)], stored.at[number]).wait()


SMEM = pl.BlockSpec(memory_space=pltpu.SMEM)
VMEM = pl.BlockSpec(memory_space=pltpu.VMEM)
ANY = pl.BlockSpec(memory_space=pl.ANY)


def f32(*shape):
    return jax.ShapeDtypeStruct(shape, jnp.float32)


def call(kernel, out_shape, in_specs, out_specs, scratch, products, aliases=None):
    return pl.pallas_call(
        kernel,
        out_shape=out_shape,
        in_specs=in_specs,
        out_specs=out_specs,
        scratch_shapes=scratch,
        input_output_aliases=aliases or {},
        cost_estimate=pl.CostEstimate(
            flops=products * 3 * 2 * BLOCK**3, bytes_accessed=4 * 1024 * 1024, transcendentals=0
        ),
        compiler_params=pltpu.CompilerParams(vmem_limit_bytes=VMEM_LIMIT),
    )


def device(r, c):
    return r * 32 + c


def tree_pairs(sources, targets):
    pairs = []
    for c in range(32):
        z, h = c // 4, c // 2 % 2
        for (a, b), (d, e) in zip(sources, targets):
            pairs.append((device((z + a) % 8 * 2 + (h ^ b), c), device((z + d) % 8 * 2 + (h ^ e), c)))
    return pairs


def send(x, pairs):
    return lax.ppermute(x, AXES, pairs)


HOLDERS = [(0, 0), (4, 0), (2, 1), (6, 1)]
FIRST = [tree_pairs([(0, 0)], [target]) for target in HOLDERS[1:]]
SECOND = [
    tree_pairs(HOLDERS, [((z + step) % 8, h ^ flip) for z, h in HOLDERS]) for step, flip in ((0, 1), (1, 0), (7, 0))
]
TRANSPOSED = [(device(r, c), device(c // 2, 2 * r + c % 2)) for r in range(16) for c in range(32)]
CORES = [(device(r, c), device(r, c ^ 1)) for r in range(16) for c in range(32)]
CHIPS = [
    (device(r, c), device(r, d)) for r in range(16) for c in range(32) for d in [c - 1 + 2 * (c % 2)] if 0 <= d < 32
]
ROWS_A = [(device(r, c), device(r ^ 1, c)) for r in range(16) for c in range(32)]
ROWS_B = [
    (device(r, c), device(q, c)) for r in range(16) for c in range(32) for q in [r - 1 + 2 * (r % 2)] if 0 <= q < 16
]


def body(matrix, moves):
    r, c = lax.axis_index("row"), lax.axis_index("col")
    rows = matrix.shape[0]
    row_odd, col_odd = r % 2, c % 2
    order = moves[0]
    slots = jnp.arange(order.shape[0], dtype=jnp.int32)
    origin = jnp.sum(jnp.where(order[None, :] == slots[:, None], slots[None, :], 0), axis=1)

    upper = lax.dynamic_slice(matrix, (col_odd * SPAN, BLOCK), (BLOCK, BLOCK))
    token = jnp.where(r == c // 2, upper, sum(send(upper, pairs) for pairs in FIRST))
    token = token + sum(send(token, pairs) for pairs in SECOND)

    mine = send(token, TRANSPOSED)
    other = send(mine, CORES)

    parity = jnp.reshape(col_odd, (1,)).astype(jnp.int32)
    away, near = call(
        columns_kernel,
        (f32(rows, BLOCK), f32(rows, BLOCK)),
        [SMEM, ANY, VMEM],
        (ANY, ANY),
        [
            pltpu.VMEM((rows, SPAN), jnp.float32),
            pltpu.VMEM((rows, SPAN), jnp.float32),
            pltpu.SemaphoreType.DMA((rows // BLOCK,)),
            pltpu.SemaphoreType.DMA((2 * rows // BLOCK,)),
        ],
        13 + 16,
    )(parity, matrix, token)
    from_chip, from_core = send(away, CHIPS), send(near, CORES)

    half = jax.ShapeDtypeStruct((2, SPAN, SPAN), jnp.bfloat16)
    high, low = call(rotations_kernel, (half, half), [SMEM, VMEM, VMEM], (VMEM, VMEM), [], 26)(parity, mine, other)

    wanted = lax.dynamic_slice_in_dim(origin, 2 * c, 2) - 2 * c + 1
    table = jnp.where(col_odd == 0, jnp.array([2, 0, 1, 3]), jnp.array([3, 1, 0, 2])).astype(jnp.int32)
    chosen = jnp.concatenate([table[wanted], jnp.reshape(row_odd, (1,)).astype(jnp.int32)])
    columns = (away, near, from_chip, from_core)
    send_a, send_b = call(
        edge_rows_kernel,
        (f32(BLOCK, SPAN), f32(BLOCK, SPAN)),
        [SMEM] + [ANY] * 4 + [VMEM] * 2,
        (ANY, ANY),
        [
            pltpu.VMEM((rows, SPAN), jnp.float32),
            pltpu.VMEM((2, BLOCK, SPAN), jnp.float32),
            pltpu.SemaphoreType.DMA((4,)),
            pltpu.SemaphoreType.DMA((2,)),
        ],
        8,
    )(chosen, *columns, high, low)
    got_a, got_b = send(send_a, ROWS_A), send(send_b, ROWS_B)

    near_slots = 4 * r - 1 + jnp.arange(6, dtype=jnp.int32)
    known = (near_slots >= 0) & (near_slots < order.shape[0])
    target = order[jnp.clip(near_slots, 0, order.shape[0] - 1)] - 4 * r
    place = jnp.where(known & (target >= 0) & (target < 4), target, -1).astype(jnp.int32)
    partial = call(
        inner_rows_kernel,
        f32(rows, SPAN),
        [SMEM] * 2 + [ANY] * 4 + [VMEM] * 2 + [ANY] * 2,
        ANY,
        [
            pltpu.VMEM((rows, SPAN), jnp.float32),
            pltpu.VMEM((2, BLOCK, SPAN), jnp.float32),
            pltpu.SemaphoreType.DMA((4,)),
            pltpu.SemaphoreType.DMA((4,)),
        ],
        8,
    )(chosen, place[1:5], *columns, high, low, send_a, send_b)
    arrived = jnp.where(row_odd == 0, place[jnp.array([5, 0])], place[jnp.array([0, 5])])
    return call(
        arrivals_kernel,
        f32(rows, SPAN),
        [SMEM] + [ANY] * 3,
        ANY,
        [pltpu.SemaphoreType.DMA((2,))],
        0,
        aliases={3: 0},
    )(arrived, got_a, got_b, partial)


def solution(mesh):
    placed = (P("row", "col"), P())
    return jax.shard_map(body, mesh=mesh, in_specs=placed, out_specs=P("row", "col"), check_vma=False)
```

time: 523 us -> 154 us (0.29)
  the two profiles are of different devices: /device:TPU:37 before, /device:TPU:142 now
where the time goes in v1:
time: 154 us
  waiting for transfers between devices  66 us (43%)
  Pallas kernels  51.9 us (34%)
  starting transfers between devices  26 us (17%)
  local copies, waits for them, and re-layouts  7.65 us (5%)
  other arithmetic  2.08 us (1%)
    ppermute x12, waiting for transfers between devices, send(): return lax.ppermute(x, AXES, pairs)  66 us
    pallas_call x1, Pallas kernels, body(): call(arrivals_kernel, f32(rows, SPAN), [SMEM] + [ANY] * 3, ANY, [pltpu.Se...  33.4 us
    ppermute x12, starting transfers between devices, send(): return lax.ppermute(x, AXES, pairs)  26 us
    pallas_call x1, Pallas kernels, body(): call(columns_kernel, (f32(rows, BLOCK), f32(rows, BLOCK)), [SMEM, ANY, VM...  6.66 us
    pallas_call x1, Pallas kernels, body(): call(rotations_kernel, (half, half), [SMEM, VMEM, VMEM], (VMEM, VMEM), []...  4.24 us
    unnamed x14, local copies, waits for them, and re-layouts  4.06 us
    pallas_call x1, Pallas kernels, body(): call(edge_rows_kernel, (f32(BLOCK, SPAN), f32(BLOCK, SPAN)), [SMEM] + [AN...  3.8 us
    pallas_call x1, Pallas kernels, body(): call(inner_rows_kernel, f32(rows, SPAN), [SMEM] * 2 + [ANY] * 4 + [VMEM]...  3.76 us
  transfers between devices with their start and end apart: 12, of which 4 were waited for; matrix products, arithmetic and copies ran while one was open for 2% of the time, Pallas kernels for 5%

profile of v1, /device:TPU:142, one launch (start us, length us, event | category | flops | bytes accessed | tf_op | source)
XLA Modules:
  0.0 153.9 jit_solution(13816274626694247537)
XLA Ops:
  0.0 1.0 constant_dynamic-slice_fusion
  1.0 0.7 collective-permute-start.2
  1.7 0.7 collective-permute-start.1
  2.3 0.7 collective-permute-start
  3.0 0.0 collective-permute-done.2
  3.1 0.0 collective-permute-done.1
  3.1 0.0 collective-permute-done
  3.1 1.0 add_select_fusion
  4.1 0.7 collective-permute-start.5
  4.8 1.3 collective-permute-start.4
  6.1 0.7 collective-permute-start.3
  6.8 0.7 broadcast_select_fusion
  7.5 0.0 collective-permute-done.5
  7.5 24.3 %collective-permute-done.4 = f32[256,256]{1,0:T(8,128)S(1)} collective-permute-done((f32[256,256]{1,0:T(8,128)S(1)}, f32[256,256]{1,0:T(8,128)S(1)}, u32[]{:S(2)}, u32[]{:S(2)}) %collective-permute-start.4) | collective-permute-done | bytes 262176 | tf_op jit(solution)/shard_map/ppermute | solution.py:221
  31.7 0.0 collective-permute-done.3
  31.7 0.1 add_add_fusion.token
  31.8 0.0 copy-start.4
  31.8 1.6 %copy-done.4 = f32[1024,512]{1,0:T(8,128)S(1)} copy-done((f32[1024,512]{1,0:T(8,128)S(1)}, f32[1024,512]{1,0:T(8,128)}, u32[]{:S(2)}) %copy-start.4) | copy-done | bytes 2097176
  33.4 0.0 copy-start.5
  33.4 6.7 %shard_map.64 = (f32[1024,256]{1,0:T(8,128)S(1)}, f32[1024,256]{1,0:T(8,128)S(1)}) custom-call(s32[1]{0:T(128)} %bitcast.3.parity, f32[1024,512]{1,0:T(8,128)S(1)} %copy-done.4, f32[256,256]{1,0:T(8,128)S(1)} %add_add_fusion.token), custom_call_target="tpu_custom_call" | custom-call | flops 2919235584 | bytes 4194304 | tf_op jit(solution)/shard_map/pallas_call | solution.py:256
  40.1 1.9 %collective-permute-start.6 = (f32[1024,256]{1,0:T(8,128)S(1)}, f32[1024,256]{1,0:T(8,128)S(1)}, u32[]{:S(2)}, u32[]{:S(2)}) collective-permute-start(f32[1024,256]{1,0:T(8,128)S(1)} %get-tuple-element.11.s0), channel_id=1, source_target_pairs={{1,2},{2,1},{3,4},{4,3},{5,6},{6,5},{7,8},{8,7},{9,10},{10,9},{11,... | collective-permute-start | bytes 3145736 | tf_op jit(solution)/shard_map/ppermute | solution.py:221
  42.0 5.6 %collective-permute-start.7 = (f32[1024,256]{1,0:T(8,128)S(1)}, f32[1024,256]{1,0:T(8,128)}, u32[]{:S(2)}, u32[]{:S(2)}) collective-permute-start(f32[1024,256]{1,0:T(8,128)S(1)} %get-tuple-element.12.s1), channel_id=1, source_target_pairs={{0,1},{1,0},{2,3},{3,2},{4,5},{5,4},{6,7},{7,6},{8,9},{9,8},{10,11... | collective-permute-start | bytes 3145736 | tf_op jit(solution)/shard_map/ppermute | solution.py:221
  47.6 0.0 copy-done.5
  47.6 0.1 select_reduce_fusion
  47.7 0.1 compare_select_fusion
  47.8 1.9 %collective-permute-start.8 = (f32[256,256]{1,0:T(8,128)S(1)}, f32[256,256]{1,0:T(8,128)}, u32[]{:S(2)}, u32[]{:S(2)}) collective-permute-start(f32[256,256]{1,0:T(8,128)S(1)} %add_add_fusion.token), channel_id=1, source_target_pairs={{0,0},{1,1},{2,32},{3,33},{4,64},{5,65},{6,96},{7,97},{8,128},{9,1... | collective-permute-start | bytes 786440 | tf_op jit(solution)/shard_map/ppermute | solution.py:221
  49.7 0.6 gather_fusion.3
  50.4 24.4 %collective-permute-done.8.mine = f32[256,256]{1,0:T(8,128)} collective-permute-done((f32[256,256]{1,0:T(8,128)S(1)}, f32[256,256]{1,0:T(8,128)}, u32[]{:S(2)}, u32[]{:S(2)}) %collective-permute-start.8) | collective-permute-done | bytes 262176 | tf_op jit(solution)/shard_map/ppermute | solution.py:221
  74.8 7.0 %collective-permute-start.9 = (f32[256,256]{1,0:T(8,128)}, f32[256,256]{1,0:T(8,128)S(1)}, u32[]{:S(2)}, u32[]{:S(2)}) collective-permute-start(f32[256,256]{1,0:T(8,128)} %collective-permute-done.8.mine), channel_id=1, source_target_pairs={{0,1},{1,0},{2,3},{3,2},{4,5},{5,4},{6,7},{7,6},{8,9},{9,8},{10,11... | collective-permute-start | bytes 786440 | tf_op jit(solution)/shard_map/ppermute | solution.py:221
  81.8 0.1 pad_add_fusion.chosen
  81.9 0.6 gather_fusion
  82.6 0.6 collective-permute-done.9.other
  83.2 4.2 %shard_map.65 = (bf16[2,512,512]{2,1,0:T(8,128)(2,1)S(1)}, bf16[2,512,512]{2,1,0:T(8,128)(2,1)S(1)}) custom-call(s32[1]{0:T(128)} %bitcast.3.parity, f32[256,256]{1,0:T(8,128)} %collective-permute-done.8.mine, f32[256,256]{1,0:T(8,128)S(1)} %collective-permute-done.9.other), custom_call_target="tpu_custom_call" | custom-call | flops 2617245696 | bytes 4194304 | tf_op jit(solution)/shard_map/pallas_call | solution.py:272
  87.4 0.0 copy-start
  87.5 0.0 copy-start.2
  87.5 0.0 collective-permute-done.6.s2
  87.5 0.0 collective-permute-done.7.s3
  87.5 0.0 copy-start.6
  87.5 3.8 %shard_map.66 = (f32[256,512]{1,0:T(8,128)}, f32[256,512]{1,0:T(8,128)}) custom-call(s32[3]{0:T(128)S(1)} %pad_add_fusion.chosen, f32[1024,256]{1,0:T(8,128)S(1)} %get-tuple-element.11.s0, f32[1024,256]{1,0:T(8,128)S(1)} %get-tuple-element.12.s1, f32[1024,256]{1,0:T(8,128)S(1)} %collective-permute-done.6.s2, f32[1024,256]{1,0:T(8,128)} %collective-permute-done.7.s3, ...), custom_call_target="tpu_custom_call" | custom-call | flops 805306368 | bytes 4194304 | tf_op jit(solution)/shard_map/pallas_call | solution.py:278
  91.3 0.0 copy-done
  91.3 0.0 copy-done.2
  91.3 2.9 %collective-permute-start.10 = (f32[256,512]{1,0:T(8,128)}, f32[256,512]{1,0:T(8,128)}, u32[]{:S(2)}, u32[]{:S(2)}) collective-permute-start(f32[256,512]{1,0:T(8,128)} %get-tuple-element.15.send_a), channel_id=1, source_target_pairs={{0,32},{1,33},{2,34},{3,35},{4,36},{5,37},{6,38},{7,39},{8,40},{9,... | collective-permute-start | bytes 1572872 | tf_op jit(solution)/shard_map/ppermute | solution.py:221
  94.2 1.9 %collective-permute-start.11 = (f32[256,512]{1,0:T(8,128)}, f32[256,512]{1,0:T(8,128)}, u32[]{:S(2)}, u32[]{:S(2)}) collective-permute-start(f32[256,512]{1,0:T(8,128)} %get-tuple-element.16.send_b), channel_id=1, source_target_pairs={{32,64},{33,65},{34,66},{35,67},{36,68},{37,69},{38,70},{39,71},{4... | collective-permute-start | bytes 1572872 | tf_op jit(solution)/shard_map/ppermute | solution.py:221
  96.2 0.1 slice.3.place
  96.3 0.6 gather_fusion.2
  96.9 0.0 copy-done.6
  96.9 0.6 gather_fusion.1
  97.6 0.0 copy-start.1
  97.6 1.2 copy-done.1
  98.8 0.0 copy-start.3
  98.8 1.2 copy-done.3
  100.0 3.8 %shard_map.67.partial = f32[1024,512]{1,0:T(8,128)} custom-call(s32[3]{0:T(128)S(1)} %pad_add_fusion.chosen, s32[4]{0:T(128)S(1)} %slice.3.place, f32[1024,256]{1,0:T(8,128)S(1)} %get-tuple-element.11.s0, f32[1024,256]{1,0:T(8,128)S(1)} %get-tuple-element.12.s1, f32[1024,256]{1,0:T(8,128)S(1)} %collective-permute-done.6.s2, ...), custom_call_target="tpu_custom_call" | custom-call | flops 805306368 | bytes 4194304 | tf_op jit(solution)/shard_map/pallas_call | solution.py:297
  103.8 16.7 %collective-permute-done.10.got_a = f32[256,512]{1,0:T(8,128)} collective-permute-done((f32[256,512]{1,0:T(8,128)}, f32[256,512]{1,0:T(8,128)}, u32[]{:S(2)}, u32[]{:S(2)}) %collective-permute-start.10) | collective-permute-done | bytes 524320 | tf_op jit(solution)/shard_map/ppermute | solution.py:221
  120.5 0.0 collective-permute-done.11.got_b
  120.5 33.4 %shard_map.68 = f32[1024,512]{1,0:T(8,128)} custom-call(s32[2]{0:T(128)S(1)} %broadcast_select_fusion.1.place, f32[256,512]{1,0:T(8,128)} %collective-permute-done.10.got_a, f32[256,512]{1,0:T(8,128)} %collective-permute-done.11.got_b, f32[1024,512]{1,0:T(8,128)} %shard_map.67.partial), custom_call_target="tpu_custom_call", output_to_operand_aliasing={{}: (3, {})} | custom-call | bytes 4194304 | tf_op jit(solution)/shard_map/pallas_call | solution.py:311
  (8 shorter events, 0.1 us)
Async XLA Ops:
  1.0 2.1 %collective-permute-start.2 = (f32[256,256]{1,0:T(8,128)S(1)}, f32[256,256]{1,0:T(8,128)S(1)}, u32[]{:S(2)}, u32[]{:S(2)}) collective-permute-start(f32[256,256]{1,0:T(8,128)S(1)} %constant_dynamic-slice_fusion), channel_id=1, source_target_pairs={{0,416},{1,417},{34,386},{35,387},{68,484},{69,485},{102,454},{103... | collective-permute-start | bytes 786440 | tf_op jit(solution)/shard_map/ppermute | solution.py:221
  1.7 1.4 collective-permute-start.1
  2.3 0.7 collective-permute-start
  4.1 3.3 %collective-permute-start.5 = (f32[256,256]{1,0:T(8,128)S(1)}, f32[256,256]{1,0:T(8,128)S(1)}, u32[]{:S(2)}, u32[]{:S(2)}) collective-permute-start(f32[256,256]{1,0:T(8,128)S(1)} %add_select_fusion), channel_id=1, source_target_pairs={{0,448},{256,192},{160,96},{416,352},{1,449},{257,193},{161,97},{4... | collective-permute-start | bytes 786440 | tf_op jit(solution)/shard_map/ppermute | solution.py:221
  4.8 26.9 %collective-permute-start.4 = (f32[256,256]{1,0:T(8,128)S(1)}, f32[256,256]{1,0:T(8,128)S(1)}, u32[]{:S(2)}, u32[]{:S(2)}) collective-permute-start(f32[256,256]{1,0:T(8,128)S(1)} %add_select_fusion), channel_id=1, source_target_pairs={{0,64},{256,320},{160,224},{416,480},{1,65},{257,321},{161,225},{4... | collective-permute-start | bytes 786440 | tf_op jit(solution)/shard_map/ppermute | solution.py:221
  6.1 25.6 %collective-permute-start.3 = (f32[256,256]{1,0:T(8,128)S(1)}, f32[256,256]{1,0:T(8,128)S(1)}, u32[]{:S(2)}, u32[]{:S(2)}) collective-permute-start(f32[256,256]{1,0:T(8,128)S(1)} %add_select_fusion), channel_id=1, source_target_pairs={{0,32},{256,288},{160,128},{416,384},{1,33},{257,289},{161,129},{4... | collective-permute-start | bytes 786440 | tf_op jit(solution)/shard_map/ppermute | solution.py:221
  31.8 1.6 %copy-start.4 = (f32[1024,512]{1,0:T(8,128)S(1)}, f32[1024,512]{1,0:T(8,128)}, u32[]{:S(2)}) copy-start(f32[1024,512]{1,0:T(8,128)} %matrix.1) | copy-start | bytes 6291460
  33.4 14.2 %copy-start.5 = (s32[1,64]{1,0:T(1,128)S(1)}, s32[1,64]{1,0:T(1,128)}, u32[]{:S(2)}) copy-start(s32[1,64]{1,0:T(1,128)} %param.7) | copy-start | bytes 772
  40.1 47.4 %collective-permute-start.6 = (f32[1024,256]{1,0:T(8,128)S(1)}, f32[1024,256]{1,0:T(8,128)S(1)}, u32[]{:S(2)}, u32[]{:S(2)}) collective-permute-start(f32[1024,256]{1,0:T(8,128)S(1)} %get-tuple-element.11.s0), channel_id=1, source_target_pairs={{1,2},{2,1},{3,4},{4,3},{5,6},{6,5},{7,8},{8,7},{9,10},{10,9},{11,... | collective-permute-start | bytes 3145736 | tf_op jit(solution)/shard_map/ppermute | solution.py:221
  42.0 45.5 %collective-permute-start.7 = (f32[1024,256]{1,0:T(8,128)S(1)}, f32[1024,256]{1,0:T(8,128)}, u32[]{:S(2)}, u32[]{:S(2)}) collective-permute-start(f32[1024,256]{1,0:T(8,128)S(1)} %get-tuple-element.12.s1), channel_id=1, source_target_pairs={{0,1},{1,0},{2,3},{3,2},{4,5},{5,4},{6,7},{7,6},{8,9},{9,8},{10,11... | collective-permute-start | bytes 3145736 | tf_op jit(solution)/shard_map/ppermute | solution.py:221
  47.8 27.0 %collective-permute-start.8 = (f32[256,256]{1,0:T(8,128)S(1)}, f32[256,256]{1,0:T(8,128)}, u32[]{:S(2)}, u32[]{:S(2)}) collective-permute-start(f32[256,256]{1,0:T(8,128)S(1)} %add_add_fusion.token), channel_id=1, source_target_pairs={{0,0},{1,1},{2,32},{3,33},{4,64},{5,65},{6,96},{7,97},{8,128},{9,1... | collective-permute-start | bytes 786440 | tf_op jit(solution)/shard_map/ppermute | solution.py:221
  74.8 8.4 %collective-permute-start.9 = (f32[256,256]{1,0:T(8,128)}, f32[256,256]{1,0:T(8,128)S(1)}, u32[]{:S(2)}, u32[]{:S(2)}) collective-permute-start(f32[256,256]{1,0:T(8,128)} %collective-permute-done.8.mine), channel_id=1, source_target_pairs={{0,1},{1,0},{2,3},{3,2},{4,5},{5,4},{6,7},{7,6},{8,9},{9,8},{10,11... | collective-permute-start | bytes 786440 | tf_op jit(solution)/shard_map/ppermute | solution.py:221
  87.4 3.9 %copy-start = (bf16[2,512,512]{2,1,0:T(8,128)(2,1)}, bf16[2,512,512]{2,1,0:T(8,128)(2,1)S(1)}, u32[]{:S(2)}) copy-start(bf16[2,512,512]{2,1,0:T(8,128)(2,1)S(1)} %get-tuple-element.13.high) | copy-start | bytes 3145732
  87.5 3.9 %copy-start.2 = (bf16[2,512,512]{2,1,0:T(8,128)(2,1)}, bf16[2,512,512]{2,1,0:T(8,128)(2,1)S(1)}, u32[]{:S(2)}) copy-start(bf16[2,512,512]{2,1,0:T(8,128)(2,1)S(1)} %get-tuple-element.14.low) | copy-start | bytes 3145732
  87.5 9.4 %copy-start.6 = (s32[2]{0:T(128)S(1)}, s32[2]{0:T(128)}, u32[]{:S(2)}) copy-start(s32[2]{0:T(128)} %constant.80) | copy-start | bytes 28
  91.3 29.2 %collective-permute-start.10 = (f32[256,512]{1,0:T(8,128)}, f32[256,512]{1,0:T(8,128)}, u32[]{:S(2)}, u32[]{:S(2)}) collective-permute-start(f32[256,512]{1,0:T(8,128)} %get-tuple-element.15.send_a), channel_id=1, source_target_pairs={{0,32},{1,33},{2,34},{3,35},{4,36},{5,37},{6,38},{7,39},{8,40},{9,... | collective-permute-start | bytes 1572872 | tf_op jit(solution)/shard_map/ppermute | solution.py:221
  94.2 26.2 %collective-permute-start.11 = (f32[256,512]{1,0:T(8,128)}, f32[256,512]{1,0:T(8,128)}, u32[]{:S(2)}, u32[]{:S(2)}) collective-permute-start(f32[256,512]{1,0:T(8,128)} %get-tuple-element.16.send_b), channel_id=1, source_target_pairs={{32,64},{33,65},{34,66},{35,67},{36,68},{37,69},{38,70},{39,71},{4... | collective-permute-start | bytes 1572872 | tf_op jit(solution)/shard_map/ppermute | solution.py:221
  97.6 1.2 copy-start.1
  98.8 1.2 copy-start.3

commit v2 on v1

v2 whole, which is shorter than its diff:
```python
import functools
import math

import jax
import jax.numpy as jnp
from jax import lax
from jax.experimental import pallas as pl
from jax.experimental.pallas import tpu as pltpu
from jax.sharding import PartitionSpec as P

BLOCK = 256
SPAN = 2 * BLOCK
AXES = ("row", "col")
VMEM_LIMIT = 32 * 1024 * 1024


def split(x):
    high = x.astype(jnp.bfloat16)
    low = (x - high.astype(jnp.float32)).astype(jnp.bfloat16)
    return high, low


def mul(a, b):
    dot = functools.partial(jnp.dot, preferred_element_type=jnp.float32)
    return dot(a[0], b[0]) + (dot(a[0], b[1]) + dot(a[1], b[0]))


def identity():
    rows = lax.broadcasted_iota(jnp.int32, (BLOCK, BLOCK), 0)
    columns = lax.broadcasted_iota(jnp.int32, (BLOCK, BLOCK), 1)
    return jnp.where(rows == columns, 1.0, 0.0).astype(jnp.float32)


def factors(uppers):
    eye = identity()
    first = 1.0 / math.sqrt(5.0)
    alpha, beta = 1.5 * first, -0.5 * first**3
    couplings, grams = [], []
    for upper in uppers:
        total = jnp.sum(jnp.sum(upper * upper, axis=1, keepdims=True), axis=0, keepdims=True)
        coupling = upper * lax.rsqrt(total / BLOCK + 1e-06)
        here, turned = split(coupling), split(coupling.T)
        couplings.append(here)
        grams.append(eye + mul(here, turned))
        grams.append(eye + mul(turned, here))
    parts = [split(gram) for gram in grams]
    squares = [mul(part, part) for part in parts]
    square_parts = [split(square) for square in squares]
    inner = [
        split(1.5 * alpha * beta**2 * gram + 0.5 * beta**3 * square) for gram, square in zip(grams, squares)
    ]
    seconds = [
        1.5 * alpha * eye + (1.5 * beta - 0.5 * alpha**3) * gram - 1.5 * alpha**2 * beta * square - mul(part, rest)
        for gram, square, part, rest in zip(grams, squares, square_parts, inner)
    ]
    second_parts = [split(second) for second in seconds]
    twice = [split(mul(part, part)) for part in second_parts]
    scaled = [split(mul(gram, part)) for gram, part in zip(parts, second_parts)]
    roots = [1.5 * second - 0.5 * mul(a, b) for second, a, b in zip(seconds, twice, scaled)]
    results = []
    for number, coupling in enumerate(couplings):
        left, right = roots[2 * number], roots[2 * number + 1]
        cross = mul(split(left), coupling)
        results.append((left, cross, cross.T, right))
    return results


def first_columns_kernel(matrix, token, away, near, high, low, held, loaded):
    load = pltpu.make_async_copy(matrix.at[pl.ds(0, SPAN)], held, loaded)
    load.start()
    left, cross, crossed, right = factors([token[...]])[0]
    even = lax.axis_index("col") % 2 == 0
    first = jnp.concatenate([left, crossed], axis=0)
    second = jnp.concatenate([-cross, right], axis=0)
    turn = split(jnp.concatenate([jnp.where(even, first, second), jnp.where(even, second, first)], axis=1))
    high[...], low[...] = turn
    load.wait()
    turned = mul(split(held[...]), turn)
    away[...] = turned[:, :BLOCK]
    near[...] = turned[:, BLOCK:]


def more_columns_kernel(matrix, high, low, away, near, held, loaded):
    load = pltpu.make_async_copy(matrix.at[pl.ds(SPAN, SPAN)], held, loaded)
    load.start()
    load.wait()
    turned = mul(split(held[...]), (high[...], low[...]))
    away[...] = turned[:, :BLOCK]
    near[...] = turned[:, BLOCK:]


def rotations_kernel(mine, other, high, low):
    even = lax.axis_index("col") % 2 == 0
    uppers = [jnp.where(even, mine[...], other[...]), jnp.where(even, other[...], mine[...])]
    for member, (left, cross, crossed, right) in enumerate(factors(uppers)):
        parts = split(
            jnp.concatenate(
                [jnp.concatenate([left, cross], axis=1), jnp.concatenate([-crossed, right], axis=1)], axis=0
            )
        )
        high[member], low[member] = parts


def rows_kernel(pair, moves, away, near, from_chip, from_core, high, low, upper, lower, held):
    c = lax.axis_index("col")
    odd = c % 2
    for slot, source in (
        (2 * c + odd, away),
        (2 * c + 1 - odd, near),
        (2 * c - 1 + 3 * odd, from_chip),
        (2 * c + 2 - 3 * odd, from_core),
    ):
        known = (slot >= 0) & (slot < moves.shape[1])
        target = moves[0, jnp.clip(slot, 0, moves.shape[1] - 1)] - 2 * c
        for half in range(2):

            @pl.when(known & (target == half))
            def _():
                held[:, half * BLOCK : (half + 1) * BLOCK] = source[...]

    turned = mul((high[pair], low[pair]), split(held[...]))
    upper[...] = turned[:BLOCK]
    lower[...] = turned[BLOCK:]


def place_kernel(moves, b0, b1, b2, b3, b4, b5, result, stored):
    r = lax.axis_index("row")

    def copies(act):
        for number, block in enumerate((b0, b1, b2, b3, b4, b5)):
            slot = 4 * r - 1 + number
            known = (slot >= 0) & (slot < moves.shape[1])
            target = moves[0, jnp.clip(slot, 0, moves.shape[1] - 1)] - 4 * r

            @pl.when(known & (target >= 0) & (target < 4))
            def _():
                spot = pl.multiple_of(jnp.clip(target, 0, 3) * BLOCK, BLOCK)
                act(pltpu.make_async_copy(block, result.at[pl.ds(spot, BLOCK)], stored.at[number]))

    copies(lambda copy: copy.start())
    copies(lambda copy: copy.wait())


SMEM = pl.BlockSpec(memory_space=pltpu.SMEM)
VMEM = pl.BlockSpec(memory_space=pltpu.VMEM)
HBM = pl.BlockSpec(memory_space=pltpu.HBM)


def f32(*shape):
    return jax.ShapeDtypeStruct(shape, jnp.float32)


def bf16(*shape):
    return jax.ShapeDtypeStruct(shape, jnp.bfloat16)


def call(kernel, out_shape, in_specs, out_specs, scratch, products):
    return pl.pallas_call(
        kernel,
        out_shape=out_shape,
        in_specs=in_specs,
        out_specs=out_specs,
        scratch_shapes=scratch,
        cost_estimate=pl.CostEstimate(
            flops=products * 3 * 2 * BLOCK**3, bytes_accessed=2 * 1024 * 1024, transcendentals=0
        ),
        compiler_params=pltpu.CompilerParams(vmem_limit_bytes=VMEM_LIMIT),
    )


def device(r, c):
    return r * 32 + c


def over_rows(sources, targets):
    pairs = []
    for c in range(32):
        z, h = c // 4, c // 2 % 2
        for (a, b), (d, e) in zip(sources, targets):
            pairs.append((device((z + a) % 8 * 2 + (h ^ b), c), device((z + d) % 8 * 2 + (h ^ e), c)))
    return pairs


def over_columns(sources, targets):
    pairs = []
    for r in range(16):
        for core in range(2):
            y, h = r // 2, r % 2
            for (a, b), (d, e) in zip(sources, targets):
                pairs.append(
                    (
                        device(r, (y + a) % 8 * 4 + (h ^ b) * 2 + core),
                        device(r, (y + d) % 8 * 4 + (h ^ e) * 2 + core),
                    )
                )
    return pairs


def send(x, pairs):
    return lax.ppermute(x, AXES, pairs)


HOLDERS = [(0, 0), (4, 0), (2, 1), (6, 1)]
STEPS = [(0, 1), (1, 0), (7, 0)]
NEXT = [[((z + step) % 8, h ^ flip) for z, h in HOLDERS] for step, flip in STEPS]
ROWS_1 = [over_rows([(0, 0)], [target]) for target in HOLDERS[1:]]
ROWS_2 = [over_rows(HOLDERS, targets) for targets in NEXT]
COLS_1 = [over_columns([(0, 0)], [target]) for target in HOLDERS[1:]]
COLS_2 = [over_columns(HOLDERS, targets) for targets in NEXT]
CORES = [(device(r, c), device(r, c ^ 1)) for r in range(16) for c in range(32)]
CHIPS = [
    (device(r, c), device(r, d)) for r in range(16) for c in range(32) for d in [c - 1 + 2 * (c % 2)] if 0 <= d < 32
]
UP = [(device(r, c), device(r - 1, c)) for r in range(1, 16) for c in range(32)]
DOWN = [(device(r, c), device(r + 1, c)) for r in range(15) for c in range(32)]


def body(matrix, moves):
    r, c = lax.axis_index("row"), lax.axis_index("col")

    upper = lax.dynamic_slice(matrix, ((c % 2) * SPAN, BLOCK), (BLOCK, BLOCK))
    owner = r == c // 2
    col_token = jnp.where(owner, upper, sum(send(upper, pairs) for pairs in ROWS_1))
    row_token = jnp.where(owner, upper, sum(send(upper, pairs) for pairs in COLS_1))
    col_token = col_token + sum(send(col_token, pairs) for pairs in ROWS_2)
    mine = row_token + sum(send(row_token, pairs) for pairs in COLS_2)
    other = send(mine, CORES)

    half = f32(SPAN, BLOCK)
    held = [pltpu.VMEM((SPAN, SPAN), jnp.float32), pltpu.SemaphoreType.DMA(())]
    away, near, high, low = call(
        first_columns_kernel,
        (half, half, bf16(SPAN, SPAN), bf16(SPAN, SPAN)),
        [HBM, VMEM],
        (VMEM,) * 4,
        held,
        13 + 8,
    )(matrix, col_token)
    parts = [(away, near, send(away, CHIPS), send(near, CORES))]
    away, near = call(more_columns_kernel, (half, half), [HBM, VMEM, VMEM], (VMEM,) * 2, held, 8)(matrix, high, low)
    parts.append((away, near, send(away, CHIPS), send(near, CORES)))

    high, low = call(rotations_kernel, (bf16(2, SPAN, SPAN),) * 2, [VMEM] * 2, (VMEM,) * 2, [], 26)(mine, other)
    wide = f32(BLOCK, SPAN)
    turn = [
        call(
            functools.partial(rows_kernel, pair),
            (wide, wide),
            [SMEM] + [VMEM] * 6,
            (VMEM,) * 2,
            [pltpu.VMEM((SPAN, SPAN), jnp.float32)],
            8,
        )
        for pair in range(2)
    ]
    first, second = turn[0](moves, *parts[0], high, low)
    below = send(first, UP)
    third, fourth = turn[1](moves, *parts[1], high, low)
    above = send(fourth, DOWN)
    return call(
        place_kernel, f32(*matrix.shape), [SMEM] + [VMEM] * 6, HBM, [pltpu.SemaphoreType.DMA((6,))], 0
    )(moves, above, first, second, third, fourth, below)


def solution(mesh):
    placed = (P("row", "col"), P())
    return jax.shard_map(body, mesh=mesh, in_specs=placed, out_specs=P("row", "col"), check_vma=False)
```

time: 154 us -> 113 us (0.73)
  the two profiles are of different devices: /device:TPU:142 before, /device:TPU:33 now
where the time goes in v2:
time: 113 us
  waiting for transfers between devices  62.4 us (55%)
  starting transfers between devices  33.5 us (30%)
  Pallas kernels  13.3 us (12%)
  local copies, waits for them, and re-layouts  1.83 us (2%)
  other arithmetic  1.28 us (1%)
    ppermute x19, waiting for transfers between devices, send(): return lax.ppermute(x, AXES, pairs)  62.4 us
    ppermute x19, starting transfers between devices, send(): return lax.ppermute(x, AXES, pairs)  33.5 us
    pallas_call x1, Pallas kernels, body(): call(first_columns_kernel, (half, half, bf16(SPAN, SPAN), bf16(SPAN, SPAN...  3.7 us
    pallas_call x1, Pallas kernels, body(): call(rotations_kernel, (bf16(2, SPAN, SPAN),) * 2, [VMEM] * 2, (VMEM,) *...  3.29 us
  transfers between devices with their start and end apart: 19, of which 6 were waited for; matrix products, arithmetic and copies ran while one was open for 0% of the time, Pallas kernels for 10%

profile of v2, /device:TPU:33, one launch (start us, length us, event | category | flops | bytes accessed | tf_op | source)
XLA Modules:
  0.0 112.7 jit_solution(1952892096224583268)
XLA Ops:
  0.0 0.0 copy-start
  0.0 1.8 %constant_dynamic-slice_fusion = f32[256,256]{1,0:T(8,128)} fusion(f32[1024,512]{1,0:T(8,128)} %matrix.3, s32[]{:T(128)S(6)} %select_n.29), kind=kLoop, calls=%fused_computation.4 | loop fusion | bytes 524292 | tf_op jit(solution)/shard_map/dynamic_slice | solution.py:221
  1.8 0.7 collective-permute-start.9
  2.5 1.3 %collective-permute-start.8 = (f32[256,256]{1,0:T(8,128)}, f32[256,256]{1,0:T(8,128)S(1)}, u32[]{:S(2)}, u32[]{:S(2)}) collective-permute-start(f32[256,256]{1,0:T(8,128)} %constant_dynamic-slice_fusion), channel_id=1, source_target_pairs={{0,16},{1,17},{34,50},{35,51},{68,84},{69,85},{102,118},{103,119},... | collective-permute-start | bytes 786440 | tf_op jit(solution)/shard_map/ppermute | solution.py:200
  3.8 0.7 collective-permute-start.10
  4.5 0.7 collective-permute-start.2
  5.2 0.7 collective-permute-start.1
  5.8 0.0 collective-permute-done.9
  5.9 1.3 %collective-permute-start = (f32[256,256]{1,0:T(8,128)}, f32[256,256]{1,0:T(8,128)}, u32[]{:S(2)}, u32[]{:S(2)}) collective-permute-start(f32[256,256]{1,0:T(8,128)} %constant_dynamic-slice_fusion), channel_id=1, source_target_pairs={{0,256},{1,257},{34,290},{35,291},{68,324},{69,325},{102,358},{103... | collective-permute-start | bytes 786440 | tf_op jit(solution)/shard_map/ppermute | solution.py:200
  7.2 9.8 %collective-permute-done.8 = f32[256,256]{1,0:T(8,128)S(1)} collective-permute-done((f32[256,256]{1,0:T(8,128)}, f32[256,256]{1,0:T(8,128)S(1)}, u32[]{:S(2)}, u32[]{:S(2)}) %collective-permute-start.8) | collective-permute-done | bytes 262176 | tf_op jit(solution)/shard_map/ppermute | solution.py:200
  17.0 0.0 collective-permute-done.10
  17.0 0.0 collective-permute-done.2
  17.0 0.0 collective-permute-done.1
  17.0 17.0 %collective-permute-done = f32[256,256]{1,0:T(8,128)} collective-permute-done((f32[256,256]{1,0:T(8,128)}, f32[256,256]{1,0:T(8,128)}, u32[]{:S(2)}, u32[]{:S(2)}) %collective-permute-start) | collective-permute-done | bytes 262176 | tf_op jit(solution)/shard_map/ppermute | solution.py:200
  34.0 1.1 %add_select_fusion = (f32[256,256]{1,0:T(8,128)S(1)}, f32[256,256]{1,0:T(8,128)S(1)}) fusion(f32[256,256]{1,0:T(8,128)S(1)} %collective-permute-done.10, f32[256,256]{1,0:T(8,128)S(1)} %collective-permute-done.8, f32[256,256]{1,0:T(8,128)S(1)} %collective-permute-done.9, pred[]{:T(512)S(6)} %eq.5, f32[256,256]{1,0:T(8,128)S(1)} %collective-permute-done.2, ...), kind=kLoop, calls=%fused_computation.1 | loop fusion | flops 393216 | bytes 2359301 | tf_op jit(solution)/shard_map/jit(_where)/select_n | solution.py:224
  35.1 1.3 %collective-permute-start.5 = (f32[256,256]{1,0:T(8,128)S(1)}, f32[256,256]{1,0:T(8,128)S(1)}, u32[]{:S(2)}, u32[]{:S(2)}) collective-permute-start(f32[256,256]{1,0:T(8,128)S(1)} %get-tuple-element.30), channel_id=1, source_target_pairs={{0,448},{256,192},{160,96},{416,352},{1,449},{257,193},{161,97},{4... | collective-permute-start | bytes 786440 | tf_op jit(solution)/shard_map/ppermute | solution.py:200
  36.4 1.3 %collective-permute-start.4 = (f32[256,256]{1,0:T(8,128)S(1)}, f32[256,256]{1,0:T(8,128)S(1)}, u32[]{:S(2)}, u32[]{:S(2)}) collective-permute-start(f32[256,256]{1,0:T(8,128)S(1)} %get-tuple-element.30), channel_id=1, source_target_pairs={{0,64},{256,320},{160,224},{416,480},{1,65},{257,321},{161,225},{4... | collective-permute-start | bytes 786440 | tf_op jit(solution)/shard_map/ppermute | solution.py:200
  37.8 1.3 %collective-permute-start.3 = (f32[256,256]{1,0:T(8,128)S(1)}, f32[256,256]{1,0:T(8,128)S(1)}, u32[]{:S(2)}, u32[]{:S(2)}) collective-permute-start(f32[256,256]{1,0:T(8,128)S(1)} %get-tuple-element.30), channel_id=1, source_target_pairs={{0,32},{256,288},{160,128},{416,384},{1,33},{257,289},{161,129},{4... | collective-permute-start | bytes 786440 | tf_op jit(solution)/shard_map/ppermute | solution.py:200
  39.1 1.3 %collective-permute-start.13 = (f32[256,256]{1,0:T(8,128)S(1)}, f32[256,256]{1,0:T(8,128)S(1)}, u32[]{:S(2)}, u32[]{:S(2)}) collective-permute-start(f32[256,256]{1,0:T(8,128)S(1)} %get-tuple-element.29), channel_id=1, source_target_pairs={{0,28},{16,12},{10,6},{26,22},{1,29},{17,13},{11,7},{27,23},{34,62... | collective-permute-start | bytes 786440 | tf_op jit(solution)/shard_map/ppermute | solution.py:200
  40.4 1.3 %collective-permute-start.12 = (f32[256,256]{1,0:T(8,128)S(1)}, f32[256,256]{1,0:T(8,128)S(1)}, u32[]{:S(2)}, u32[]{:S(2)}) collective-permute-start(f32[256,256]{1,0:T(8,128)S(1)} %get-tuple-element.29), channel_id=1, source_target_pairs={{0,4},{16,20},{10,14},{26,30},{1,5},{17,21},{11,15},{27,31},{34,38... | collective-permute-start | bytes 786440 | tf_op jit(solution)/shard_map/ppermute | solution.py:200
  41.7 0.0 collective-permute-done.5
  41.7 1.3 %collective-permute-start.11 = (f32[256,256]{1,0:T(8,128)S(1)}, f32[256,256]{1,0:T(8,128)S(1)}, u32[]{:S(2)}, u32[]{:S(2)}) collective-permute-start(f32[256,256]{1,0:T(8,128)S(1)} %get-tuple-element.29), channel_id=1, source_target_pairs={{0,2},{16,18},{10,8},{26,24},{1,3},{17,19},{11,9},{27,25},{34,32},... | collective-permute-start | bytes 786440 | tf_op jit(solution)/shard_map/ppermute | solution.py:200
  43.0 0.0 collective-permute-done.4
  43.0 0.3 collective-permute-done.3
  43.3 0.1 add_add_fusion.1.token
  43.4 0.0 copy-done
  43.4 3.7 %shard_map.28 = (f32[512,256]{1,0:T(8,128)S(1)}, f32[512,256]{1,0:T(8,128)S(1)}, bf16[512,512]{1,0:T(8,128)(2,1)S(1)}, bf16[512,512]{1,0:T(8,128)(2,1)S(1)}) custom-call(f32[1024,512]{1,0:T(8,128)S(1)} %copy-done, f32[256,256]{1,0:T(8,128)S(1)} %add_add_fusion.1.token), custom_call_target="tpu_custom_call" | custom-call | flops 2113929216 | bytes 2097152 | tf_op jit(solution)/shard_map/pallas_call | solution.py:231
  47.1 1.1 shard_map.29
  48.2 8.9 %collective-permute-start.6 = (f32[512,256]{1,0:T(8,128)S(1)}, f32[512,256]{1,0:T(8,128)S(1)}, u32[]{:S(2)}, u32[]{:S(2)}) collective-permute-start(f32[512,256]{1,0:T(8,128)S(1)} %get-tuple-element.19.away), channel_id=1, source_target_pairs={{1,2},{2,1},{3,4},{4,3},{5,6},{6,5},{7,8},{8,7},{9,10},{10,9},{11,... | collective-permute-start | bytes 1572872 | tf_op jit(solution)/shard_map/ppermute | solution.py:200
  57.1 1.9 %collective-permute-start.7 = (f32[512,256]{1,0:T(8,128)S(1)}, f32[512,256]{1,0:T(8,128)S(1)}, u32[]{:S(2)}, u32[]{:S(2)}) collective-permute-start(f32[512,256]{1,0:T(8,128)S(1)} %get-tuple-element.20.near), channel_id=1, source_target_pairs={{0,1},{1,0},{2,3},{3,2},{4,5},{5,4},{6,7},{7,6},{8,9},{9,8},{10,11... | collective-permute-start | bytes 1572872 | tf_op jit(solution)/shard_map/ppermute | solution.py:200
  59.0 0.0 collective-permute-done.13
  59.0 0.0 collective-permute-done.12
  59.0 0.0 collective-permute-done.11
  59.0 0.1 add_add_fusion.mine
  59.1 2.4 %collective-permute-start.14 = (f32[256,256]{1,0:T(8,128)S(1)}, f32[256,256]{1,0:T(8,128)S(1)}, u32[]{:S(2)}, u32[]{:S(2)}) collective-permute-start(f32[256,256]{1,0:T(8,128)S(1)} %add_add_fusion.mine), channel_id=1, source_target_pairs={{0,1},{1,0},{2,3},{3,2},{4,5},{5,4},{6,7},{7,6},{8,9},{9,8},{10,11... | collective-permute-start | bytes 786440 | tf_op jit(solution)/shard_map/ppermute | solution.py:200
  61.5 1.9 %collective-permute-start.16 = (f32[512,256]{1,0:T(8,128)S(1)}, f32[512,256]{1,0:T(8,128)S(1)}, u32[]{:S(2)}, u32[]{:S(2)}) collective-permute-start(f32[512,256]{1,0:T(8,128)S(1)} %get-tuple-element.24.away), channel_id=1, source_target_pairs={{1,2},{2,1},{3,4},{4,3},{5,6},{6,5},{7,8},{8,7},{9,10},{10,9},{11,... | collective-permute-start | bytes 1572872 | tf_op jit(solution)/shard_map/ppermute | solution.py:200
  63.5 0.0 copy-start.1
  63.5 2.6 %collective-permute-start.17 = (f32[512,256]{1,0:T(8,128)S(1)}, f32[512,256]{1,0:T(8,128)S(1)}, u32[]{:S(2)}, u32[]{:S(2)}) collective-permute-start(f32[512,256]{1,0:T(8,128)S(1)} %get-tuple-element.25.near), channel_id=1, source_target_pairs={{0,1},{1,0},{2,3},{3,2},{4,5},{5,4},{6,7},{7,6},{8,9},{9,8},{10,11... | collective-permute-start | bytes 1572872 | tf_op jit(solution)/shard_map/ppermute | solution.py:200
  66.1 0.0 collective-permute-done.14.other
  66.1 3.3 %shard_map.30 = (bf16[2,512,512]{2,1,0:T(8,128)(2,1)S(1)}, bf16[2,512,512]{2,1,0:T(8,128)(2,1)S(1)}) custom-call(f32[256,256]{1,0:T(8,128)S(1)} %add_add_fusion.mine, f32[256,256]{1,0:T(8,128)S(1)} %collective-permute-done.14.other), custom_call_target="tpu_custom_call" | custom-call | flops 2617245696 | bytes 2097152 | tf_op jit(solution)/shard_map/pallas_call | solution.py:243
  69.4 6.3 %collective-permute-done.6.from_chip = f32[512,256]{1,0:T(8,128)S(1)} collective-permute-done((f32[512,256]{1,0:T(8,128)S(1)}, f32[512,256]{1,0:T(8,128)S(1)}, u32[]{:S(2)}, u32[]{:S(2)}) %collective-permute-start.6) | collective-permute-done | bytes 524320 | tf_op jit(solution)/shard_map/ppermute | solution.py:200
  75.7 0.0 collective-permute-done.7.from_core
  75.7 0.0 copy-done.1
  75.7 1.7 %shard_map.31 = (f32[256,512]{1,0:T(8,128)S(1)}, f32[256,512]{1,0:T(8,128)S(1)}) custom-call(s32[1,64]{1,0:T(1,128)S(1)} %copy-done.1, f32[512,256]{1,0:T(8,128)S(1)} %get-tuple-element.19.away, f32[512,256]{1,0:T(8,128)S(1)} %get-tuple-element.20.near, f32[512,256]{1,0:T(8,128)S(1)} %collective-permute-done.6.from_chip, ...), custom_call_target="tpu_custom_call" | custom-call | flops 805306368 | bytes 2097152 | tf_op jit(solution)/shard_map/pallas_call | solution.py:258
  77.4 1.3 %collective-permute-start.15 = (f32[256,512]{1,0:T(8,128)S(1)}, f32[256,512]{1,0:T(8,128)S(1)}, u32[]{:S(2)}, u32[]{:S(2)}) collective-permute-start(f32[256,512]{1,0:T(8,128)S(1)} %get-tuple-element.23.b4), channel_id=1, source_target_pairs={{0,32},{1,33},{2,34},{3,35},{4,36},{5,37},{6,38},{7,39},{8,40},{9,... | collective-permute-start | bytes 1572872 | tf_op jit(solution)/shard_map/ppermute | solution.py:200
  78.7 18.9 %collective-permute-done.16.from_chip = f32[512,256]{1,0:T(8,128)S(1)} collective-permute-done((f32[512,256]{1,0:T(8,128)S(1)}, f32[512,256]{1,0:T(8,128)S(1)}, u32[]{:S(2)}, u32[]{:S(2)}) %collective-permute-start.16) | collective-permute-done | bytes 524320 | tf_op jit(solution)/shard_map/ppermute | solution.py:200
  97.6 0.0 collective-permute-done.17.from_core
  97.6 1.7 %shard_map.32 = (f32[256,512]{1,0:T(8,128)S(1)}, f32[256,512]{1,0:T(8,128)S(1)}) custom-call(s32[1,64]{1,0:T(1,128)S(1)} %copy-done.1, f32[512,256]{1,0:T(8,128)S(1)} %get-tuple-element.24.away, f32[512,256]{1,0:T(8,128)S(1)} %get-tuple-element.25.near, f32[512,256]{1,0:T(8,128)S(1)} %collective-permute-done.16.from_chip, ...), custom_call_target="tpu_custom_call" | custom-call | flops 805306368 | bytes 2097152 | tf_op jit(solution)/shard_map/pallas_call | solution.py:256
  99.3 1.3 %collective-permute-start.18 = (f32[256,512]{1,0:T(8,128)S(1)}, f32[256,512]{1,0:T(8,128)S(1)}, u32[]{:S(2)}, u32[]{:S(2)}) collective-permute-start(f32[256,512]{1,0:T(8,128)S(1)} %get-tuple-element.26.b1), channel_id=1, source_target_pairs={{32,0},{33,1},{34,2},{35,3},{36,4},{37,5},{38,6},{39,7},{40,8},{41... | collective-permute-start | bytes 1572872 | tf_op jit(solution)/shard_map/ppermute | solution.py:200
  100.6 0.0 collective-permute-done.15.b0
  100.6 10.1 %collective-permute-done.18.b5 = f32[256,512]{1,0:T(8,128)S(1)} collective-permute-done((f32[256,512]{1,0:T(8,128)S(1)}, f32[256,512]{1,0:T(8,128)S(1)}, u32[]{:S(2)}, u32[]{:S(2)}) %collective-permute-start.18) | collective-permute-done | bytes 524320 | tf_op jit(solution)/shard_map/ppermute | solution.py:200
  110.7 1.9 %shard_map.33 = f32[1024,512]{1,0:T(8,128)} custom-call(s32[1,64]{1,0:T(1,128)S(1)} %copy-done.1, f32[256,512]{1,0:T(8,128)S(1)} %collective-permute-done.15.b0, f32[256,512]{1,0:T(8,128)S(1)} %get-tuple-element.26.b1, f32[256,512]{1,0:T(8,128)S(1)} %get-tuple-element.27.b2, f32[256,512]{1,0:T(8,128)S(1)} %get-tuple-element.28.b3, ...), custom_call_target="tpu_custom_call" | custom-call | bytes 2097152 | tf_op jit(solution)/shard_map/pallas_call | solution.py:260
Async XLA Ops:
  0.0 43.4 %copy-start = (f32[1024,512]{1,0:T(8,128)S(1)}, f32[1024,512]{1,0:T(8,128)}, u32[]{:S(2)}) copy-start(f32[1024,512]{1,0:T(8,128)} %matrix.3) | copy-start | bytes 6291460
  1.8 4.0 %collective-permute-start.9 = (f32[256,256]{1,0:T(8,128)}, f32[256,256]{1,0:T(8,128)S(1)}, u32[]{:S(2)}, u32[]{:S(2)}) collective-permute-start(f32[256,256]{1,0:T(8,128)} %constant_dynamic-slice_fusion), channel_id=1, source_target_pairs={{0,10},{1,11},{34,40},{35,41},{68,78},{69,79},{102,108},{103,109},... | collective-permute-start | bytes 786440 | tf_op jit(solution)/shard_map/ppermute | solution.py:200
  2.5 14.5 %collective-permute-start.8 = (f32[256,256]{1,0:T(8,128)}, f32[256,256]{1,0:T(8,128)S(1)}, u32[]{:S(2)}, u32[]{:S(2)}) collective-permute-start(f32[256,256]{1,0:T(8,128)} %constant_dynamic-slice_fusion), channel_id=1, source_target_pairs={{0,16},{1,17},{34,50},{35,51},{68,84},{69,85},{102,118},{103,119},... | collective-permute-start | bytes 786440 | tf_op jit(solution)/shard_map/ppermute | solution.py:200
  3.8 13.2 %collective-permute-start.10 = (f32[256,256]{1,0:T(8,128)}, f32[256,256]{1,0:T(8,128)S(1)}, u32[]{:S(2)}, u32[]{:S(2)}) collective-permute-start(f32[256,256]{1,0:T(8,128)} %constant_dynamic-slice_fusion), channel_id=1, source_target_pairs={{0,26},{1,27},{34,56},{35,57},{68,94},{69,95},{102,124},{103,125},... | collective-permute-start | bytes 786440 | tf_op jit(solution)/shard_map/ppermute | solution.py:200
  4.5 12.5 %collective-permute-start.2 = (f32[256,256]{1,0:T(8,128)}, f32[256,256]{1,0:T(8,128)S(1)}, u32[]{:S(2)}, u32[]{:S(2)}) collective-permute-start(f32[256,256]{1,0:T(8,128)} %constant_dynamic-slice_fusion), channel_id=1, source_target_pairs={{0,416},{1,417},{34,386},{35,387},{68,484},{69,485},{102,454},{103... | collective-permute-start | bytes 786440 | tf_op jit(solution)/shard_map/ppermute | solution.py:200
  5.2 11.9 %collective-permute-start.1 = (f32[256,256]{1,0:T(8,128)}, f32[256,256]{1,0:T(8,128)S(1)}, u32[]{:S(2)}, u32[]{:S(2)}) collective-permute-start(f32[256,256]{1,0:T(8,128)} %constant_dynamic-slice_fusion), channel_id=1, source_target_pairs={{0,160},{1,161},{34,130},{35,131},{68,228},{69,229},{102,198},{103... | collective-permute-start | bytes 786440 | tf_op jit(solution)/shard_map/ppermute | solution.py:200
  5.9 28.1 %collective-permute-start = (f32[256,256]{1,0:T(8,128)}, f32[256,256]{1,0:T(8,128)}, u32[]{:S(2)}, u32[]{:S(2)}) collective-permute-start(f32[256,256]{1,0:T(8,128)} %constant_dynamic-slice_fusion), channel_id=1, source_target_pairs={{0,256},{1,257},{34,290},{35,291},{68,324},{69,325},{102,358},{103... | collective-permute-start | bytes 786440 | tf_op jit(solution)/shard_map/ppermute | solution.py:200
  35.1 6.6 %collective-permute-start.5 = (f32[256,256]{1,0:T(8,128)S(1)}, f32[256,256]{1,0:T(8,128)S(1)}, u32[]{:S(2)}, u32[]{:S(2)}) collective-permute-start(f32[256,256]{1,0:T(8,128)S(1)} %get-tuple-element.30), channel_id=1, source_target_pairs={{0,448},{256,192},{160,96},{416,352},{1,449},{257,193},{161,97},{4... | collective-permute-start | bytes 786440 | tf_op jit(solution)/shard_map/ppermute | solution.py:200
  36.4 6.6 %collective-permute-start.4 = (f32[256,256]{1,0:T(8,128)S(1)}, f32[256,256]{1,0:T(8,128)S(1)}, u32[]{:S(2)}, u32[]{:S(2)}) collective-permute-start(f32[256,256]{1,0:T(8,128)S(1)} %get-tuple-element.30), channel_id=1, source_target_pairs={{0,64},{256,320},{160,224},{416,480},{1,65},{257,321},{161,225},{4... | collective-permute-start | bytes 786440 | tf_op jit(solution)/shard_map/ppermute | solution.py:200
  37.8 5.6 %collective-permute-start.3 = (f32[256,256]{1,0:T(8,128)S(1)}, f32[256,256]{1,0:T(8,128)S(1)}, u32[]{:S(2)}, u32[]{:S(2)}) collective-permute-start(f32[256,256]{1,0:T(8,128)S(1)} %get-tuple-element.30), channel_id=1, source_target_pairs={{0,32},{256,288},{160,128},{416,384},{1,33},{257,289},{161,129},{4... | collective-permute-start | bytes 786440 | tf_op jit(solution)/shard_map/ppermute | solution.py:200
  39.1 19.9 %collective-permute-start.13 = (f32[256,256]{1,0:T(8,128)S(1)}, f32[256,256]{1,0:T(8,128)S(1)}, u32[]{:S(2)}, u32[]{:S(2)}) collective-permute-start(f32[256,256]{1,0:T(8,128)S(1)} %get-tuple-element.29), channel_id=1, source_target_pairs={{0,28},{16,12},{10,6},{26,22},{1,29},{17,13},{11,7},{27,23},{34,62... | collective-permute-start | bytes 786440 | tf_op jit(solution)/shard_map/ppermute | solution.py:200
  40.4 18.6 %collective-permute-start.12 = (f32[256,256]{1,0:T(8,128)S(1)}, f32[256,256]{1,0:T(8,128)S(1)}, u32[]{:S(2)}, u32[]{:S(2)}) collective-permute-start(f32[256,256]{1,0:T(8,128)S(1)} %get-tuple-element.29), channel_id=1, source_target_pairs={{0,4},{16,20},{10,14},{26,30},{1,5},{17,21},{11,15},{27,31},{34,38... | collective-permute-start | bytes 786440 | tf_op jit(solution)/shard_map/ppermute | solution.py:200
  41.7 17.3 %collective-permute-start.11 = (f32[256,256]{1,0:T(8,128)S(1)}, f32[256,256]{1,0:T(8,128)S(1)}, u32[]{:S(2)}, u32[]{:S(2)}) collective-permute-start(f32[256,256]{1,0:T(8,128)S(1)} %get-tuple-element.29), channel_id=1, source_target_pairs={{0,2},{16,18},{10,8},{26,24},{1,3},{17,19},{11,9},{27,25},{34,32},... | collective-permute-start | bytes 786440 | tf_op jit(solution)/shard_map/ppermute | solution.py:200
  48.2 27.5 %collective-permute-start.6 = (f32[512,256]{1,0:T(8,128)S(1)}, f32[512,256]{1,0:T(8,128)S(1)}, u32[]{:S(2)}, u32[]{:S(2)}) collective-permute-start(f32[512,256]{1,0:T(8,128)S(1)} %get-tuple-element.19.away), channel_id=1, source_target_pairs={{1,2},{2,1},{3,4},{4,3},{5,6},{6,5},{7,8},{8,7},{9,10},{10,9},{11,... | collective-permute-start | bytes 1572872 | tf_op jit(solution)/shard_map/ppermute | solution.py:200
  57.1 18.6 %collective-permute-start.7 = (f32[512,256]{1,0:T(8,128)S(1)}, f32[512,256]{1,0:T(8,128)S(1)}, u32[]{:S(2)}, u32[]{:S(2)}) collective-permute-start(f32[512,256]{1,0:T(8,128)S(1)} %get-tuple-element.20.near), channel_id=1, source_target_pairs={{0,1},{1,0},{2,3},{3,2},{4,5},{5,4},{6,7},{7,6},{8,9},{9,8},{10,11... | collective-permute-start | bytes 1572872 | tf_op jit(solution)/shard_map/ppermute | solution.py:200
  59.1 7.0 %collective-permute-start.14 = (f32[256,256]{1,0:T(8,128)S(1)}, f32[256,256]{1,0:T(8,128)S(1)}, u32[]{:S(2)}, u32[]{:S(2)}) collective-permute-start(f32[256,256]{1,0:T(8,128)S(1)} %add_add_fusion.mine), channel_id=1, source_target_pairs={{0,1},{1,0},{2,3},{3,2},{4,5},{5,4},{6,7},{7,6},{8,9},{9,8},{10,11... | collective-permute-start | bytes 786440 | tf_op jit(solution)/shard_map/ppermute | solution.py:200
  61.5 36.1 %collective-permute-start.16 = (f32[512,256]{1,0:T(8,128)S(1)}, f32[512,256]{1,0:T(8,128)S(1)}, u32[]{:S(2)}, u32[]{:S(2)}) collective-permute-start(f32[512,256]{1,0:T(8,128)S(1)} %get-tuple-element.24.away), channel_id=1, source_target_pairs={{1,2},{2,1},{3,4},{4,3},{5,6},{6,5},{7,8},{8,7},{9,10},{10,9},{11,... | collective-permute-start | bytes 1572872 | tf_op jit(solution)/shard_map/ppermute | solution.py:200
  63.5 12.2 %copy-start.1 = (s32[1,64]{1,0:T(1,128)S(1)}, s32[1,64]{1,0:T(1,128)}, u32[]{:S(2)}) copy-start(s32[1,64]{1,0:T(1,128)} %moves.5) | copy-start | bytes 772
  63.5 34.2 %collective-permute-start.17 = (f32[512,256]{1,0:T(8,128)S(1)}, f32[512,256]{1,0:T(8,128)S(1)}, u32[]{:S(2)}, u32[]{:S(2)}) collective-permute-start(f32[512,256]{1,0:T(8,128)S(1)} %get-tuple-element.25.near), channel_id=1, source_target_pairs={{0,1},{1,0},{2,3},{3,2},{4,5},{5,4},{6,7},{7,6},{8,9},{9,8},{10,11... | collective-permute-start | bytes 1572872 | tf_op jit(solution)/shard_map/ppermute | solution.py:200
  77.4 23.2 %collective-permute-start.15 = (f32[256,512]{1,0:T(8,128)S(1)}, f32[256,512]{1,0:T(8,128)S(1)}, u32[]{:S(2)}, u32[]{:S(2)}) collective-permute-start(f32[256,512]{1,0:T(8,128)S(1)} %get-tuple-element.23.b4), channel_id=1, source_target_pairs={{0,32},{1,33},{2,34},{3,35},{4,36},{5,37},{6,38},{7,39},{8,40},{9,... | collective-permute-start | bytes 1572872 | tf_op jit(solution)/shard_map/ppermute | solution.py:200
  99.3 11.4 %collective-permute-start.18 = (f32[256,512]{1,0:T(8,128)S(1)}, f32[256,512]{1,0:T(8,128)S(1)}, u32[]{:S(2)}, u32[]{:S(2)}) collective-permute-start(f32[256,512]{1,0:T(8,128)S(1)} %get-tuple-element.26.b1), channel_id=1, source_target_pairs={{32,0},{33,1},{34,2},{35,3},{36,4},{37,5},{38,6},{39,7},{40,8},{41... | collective-permute-start | bytes 1572872 | tf_op jit(solution)/shard_map/ppermute | solution.py:200

commit v3 on v2

--- a/solution.py
+++ b/solution.py
@@ -65,10 +65,30 @@
     return results
 
 
-def first_columns_kernel(matrix, token, away, near, high, low, held, loaded):
+def pivot_kernel(matrix, upper, loaded):
+    first = pl.multiple_of(lax.axis_index("col") % 2 * SPAN, SPAN)
+    load = pltpu.make_async_copy(matrix.at[pl.ds(first, BLOCK), pl.ds(BLOCK, BLOCK)], upper, loaded)
+    load.start()
+    load.wait()
+
+
+def again_kernel(upper, copy):
+    copy[...] = upper[...]
+
+
+def join_kernel(first, t0, t1, t2, token):
+    owner = lax.axis_index("row") == lax.axis_index("col") // 2
+    token[...] = jnp.where(owner, first[...], t0[...] + (t1[...] + t2[...]))
+
+
+def sum_kernel(first, t0, t1, t2, token):
+    token[...] = (first[...] + t0[...]) + (t1[...] + t2[...])
+
+
+def first_columns_kernel(matrix, t0, t1, t2, t3, away, near, high, low, held, loaded):
     load = pltpu.make_async_copy(matrix.at[pl.ds(0, SPAN)], held, loaded)
     load.start()
-    left, cross, crossed, right = factors([token[...]])[0]
+    left, cross, crossed, right = factors([t0[...] + ((t1[...] + t2[...]) + t3[...])])[0]
     even = lax.axis_index("col") % 2 == 0
     first = jnp.concatenate([left, crossed], axis=0)
     second = jnp.concatenate([-cross, right], axis=0)
@@ -162,7 +182,7 @@
         out_specs=out_specs,
         scratch_shapes=scratch,
         cost_estimate=pl.CostEstimate(
-            flops=products * 3 * 2 * BLOCK**3, bytes_accessed=2 * 1024 * 1024, transcendentals=0
+            flops=products * 3 * 2 * BLOCK**3, bytes_accessed=0, transcendentals=0
         ),
         compiler_params=pltpu.CompilerParams(vmem_limit_bytes=VMEM_LIMIT),
     )
@@ -202,11 +222,11 @@
 
 HOLDERS = [(0, 0), (4, 0), (2, 1), (6, 1)]
 STEPS = [(0, 1), (1, 0), (7, 0)]
-NEXT = [[((z + step) % 8, h ^ flip) for z, h in HOLDERS] for step, flip in STEPS]
 ROWS_1 = [over_rows([(0, 0)], [target]) for target in HOLDERS[1:]]
-ROWS_2 = [over_rows(HOLDERS, targets) for targets in NEXT]
-COLS_1 = [over_columns([(0, 0)], [target]) for target in HOLDERS[1:]]
-COLS_2 = [over_columns(HOLDERS, targets) for targets in NEXT]
+ROWS_2 = [over_rows(HOLDERS, [((z + step) % 8, h ^ flip) for z, h in HOLDERS]) for step, flip in STEPS]
+EVEN = [(0, 0), (4, 0), (2, 0), (6, 0)]
+COLS_1 = [over_columns([(0, 0)], [target]) for target in EVEN[1:]]
+COLS_2 = [over_columns(EVEN, [((y + step) % 8, flip) for y, _ in EVEN]) for step, flip in ((1, 0), (0, 1), (1, 1))]
 CORES = [(device(r, c), device(r, c ^ 1)) for r in range(16) for c in range(32)]
 CHIPS = [
     (device(r, c), device(r, d)) for r in range(16) for c in range(32) for d in [c - 1 + 2 * (c % 2)] if 0 <= d < 32
@@ -216,14 +236,17 @@
 
 
 def body(matrix, moves):
-    r, c = lax.axis_index("row"), lax.axis_index("col")
-
-    upper = lax.dynamic_slice(matrix, ((c % 2) * SPAN, BLOCK), (BLOCK, BLOCK))
-    owner = r == c // 2
-    col_token = jnp.where(owner, upper, sum(send(upper, pairs) for pairs in ROWS_1))
-    row_token = jnp.where(owner, upper, sum(send(upper, pairs) for pairs in COLS_1))
-    col_token = col_token + sum(send(col_token, pairs) for pairs in ROWS_2)
-    mine = row_token + sum(send(row_token, pairs) for pairs in COLS_2)
+    upper = call(
+        pivot_kernel, f32(BLOCK, BLOCK), [HBM], VMEM, [pltpu.SemaphoreType.DMA(())], 0
+    )(matrix)
+    again = call(again_kernel, f32(BLOCK, BLOCK), [VMEM], VMEM, [], 0)(upper)
+    join = call(join_kernel, f32(BLOCK, BLOCK), [VMEM] * 4, VMEM, [], 0)
+    col_token = join(upper, *[send(upper, pairs) for pairs in ROWS_1])
+    col_tokens = [col_token] + [send(col_token, pairs) for pairs in ROWS_2]
+    row_token = join(again, *[send(again, pairs) for pairs in COLS_1])
+    mine = call(sum_kernel, f32(BLOCK, BLOCK), [VMEM] * 4, VMEM, [], 0)(
+        row_token, *[send(row_token, pairs) for pairs in COLS_2]
+    )
     other = send(mine, CORES)
 
     half = f32(SPAN, BLOCK)
@@ -231,16 +254,16 @@
     away, near, high, low = call(
         first_columns_kernel,
         (half, half, bf16(SPAN, SPAN), bf16(SPAN, SPAN)),
-        [HBM, VMEM],
+        [HBM] + [VMEM] * 4,
         (VMEM,) * 4,
         held,
-        13 + 8,
-    )(matrix, col_token)
+        0,
+    )(matrix, *col_tokens)
     parts = [(away, near, send(away, CHIPS), send(near, CORES))]
-    away, near = call(more_columns_kernel, (half, half), [HBM, VMEM, VMEM], (VMEM,) * 2, held, 8)(matrix, high, low)
+    away, near = call(more_columns_kernel, (half, half), [HBM, VMEM, VMEM], (VMEM,) * 2, held, 0)(matrix, high, low)
     parts.append((away, near, send(away, CHIPS), send(near, CORES)))
 
-    high, low = call(rotations_kernel, (bf16(2, SPAN, SPAN),) * 2, [VMEM] * 2, (VMEM,) * 2, [], 26)(mine, other)
+    high, low = call(rotations_kernel, (bf16(2, SPAN, SPAN),) * 2, [VMEM] * 2, (VMEM,) * 2, [], 0)(mine, other)
     wide = f32(BLOCK, SPAN)
     turn = [
         call(
@@ -249,7 +272,7 @@
             [SMEM] + [VMEM] * 6,
             (VMEM,) * 2,
             [pltpu.VMEM((SPAN, SPAN), jnp.float32)],
-            8,
+            0,
         )
         for pair in range(2)
     ]

time: 113 us -> 99.7 us (0.88)
  the two profiles are of different devices: /device:TPU:33 before, /device:TPU:194 now
where the time goes in v3:
time: 99.7 us; the launch traced here: 99.2 us
  waiting for transfers between devices  59 us (59%)
  starting transfers between devices  24.7 us (25%)
  Pallas kernels  13.5 us (14%)
  local copies, waits for them, and re-layouts  1.6 us (2%)
    ppermute x19, waiting for transfers between devices, send(): return lax.ppermute(x, AXES, pairs)  59 us
    ppermute x19, starting transfers between devices, send(): return lax.ppermute(x, AXES, pairs)  24.7 us
    pallas_call x1, Pallas kernels, body(): call(first_columns_kernel, (half, half, bf16(SPAN, SPAN), bf16(SPAN, SPAN...  3.71 us
    pallas_call x1, Pallas kernels, body(): call(rotations_kernel, (bf16(2, SPAN, SPAN),) * 2, [VMEM] * 2, (VMEM,) *...  3.28 us
  transfers between devices with their start and end apart: 19, of which 6 were waited for; matrix products, arithmetic and copies ran while one was open for 0% of the time, Pallas kernels for 12%

profile of v3, /device:TPU:194, one launch (start us, length us, event | category | flops | bytes accessed | tf_op | source)
XLA Modules:
  0.0 99.2 jit_solution(2820531991688397381)
XLA Ops:
  0.0 0.0 copy-start
  0.0 1.6 %copy-done = f32[1024,512]{1,0:T(8,128)S(1)} copy-done((f32[1024,512]{1,0:T(8,128)S(1)}, f32[1024,512]{1,0:T(8,128)}, u32[]{:S(2)}) %copy-start) | copy-done | bytes 2097176
  1.6 0.0 copy-start.1
  1.6 0.8 collective-permute-start
  2.5 0.7 collective-permute-start.1
  3.1 0.7 collective-permute-start.2
  3.9 0.7 collective-permute-start.10
  4.5 0.7 collective-permute-start.8
  5.2 0.0 collective-permute-done.t0
  5.2 0.7 collective-permute-start.9
  5.9 0.0 collective-permute-done.1.t1
  5.9 0.0 collective-permute-done.2.t2
  5.9 0.1 shard_map.29.t0
  6.0 0.7 collective-permute-start.3
  6.7 1.3 %collective-permute-start.4 = (f32[256,256]{1,0:T(8,128)S(1)}, f32[256,256]{1,0:T(8,128)S(1)}, u32[]{:S(2)}, u32[]{:S(2)}) collective-permute-start(f32[256,256]{1,0:T(8,128)S(1)} %shard_map.29.t0), channel_id=1, source_target_pairs={{0,64},{256,320},{160,224},{416,480},{1,65},{257,321},{161,225},{4... | collective-permute-start | bytes 786440 | tf_op jit(solution)/shard_map/ppermute | solution.py:220
  8.0 0.0 collective-permute-done.10.t2
  8.0 0.7 collective-permute-start.5
  8.7 0.0 collective-permute-done.8.t0
  8.7 0.0 collective-permute-done.9.t1
  8.7 0.1 shard_map.33.first
  8.8 0.7 collective-permute-start.11
  9.5 0.7 collective-permute-start.12
  10.1 0.0 collective-permute-done.3.t1
  10.1 1.3 %collective-permute-start.13 = (f32[256,256]{1,0:T(8,128)S(1)}, f32[256,256]{1,0:T(8,128)S(1)}, u32[]{:S(2)}, u32[]{:S(2)}) collective-permute-start(f32[256,256]{1,0:T(8,128)S(1)} %shard_map.33.first), channel_id=1, source_target_pairs={{0,6},{16,22},{8,14},{24,30},{1,7},{17,23},{9,15},{25,31},{34,36},... | collective-permute-start | bytes 786440 | tf_op jit(solution)/shard_map/ppermute | solution.py:220
  11.4 20.9 %collective-permute-done.4.t2 = f32[256,256]{1,0:T(8,128)S(1)} collective-permute-done((f32[256,256]{1,0:T(8,128)S(1)}, f32[256,256]{1,0:T(8,128)S(1)}, u32[]{:S(2)}, u32[]{:S(2)}) %collective-permute-start.4) | collective-permute-done | bytes 262176 | tf_op jit(solution)/shard_map/ppermute | solution.py:220
  32.4 0.0 collective-permute-done.5.t3
  32.4 0.0 copy-done.1
  32.4 3.7 %shard_map.30 = (f32[512,256]{1,0:T(8,128)S(1)}, f32[512,256]{1,0:T(8,128)S(1)}, bf16[512,512]{1,0:T(8,128)(2,1)S(1)}, bf16[512,512]{1,0:T(8,128)(2,1)S(1)}) custom-call(f32[1024,512]{1,0:T(8,128)S(1)} %copy-done.1, f32[256,256]{1,0:T(8,128)S(1)} %shard_map.29.t0, f32[256,256]{1,0:T(8,128)S(1)} %collective-permute-done.3.t1, ...), custom_call_target="tpu_custom_call" | custom-call | tf_op jit(solution)/shard_map/pallas_call | solution.py:254
  36.1 1.9 %collective-permute-start.16 = (f32[512,256]{1,0:T(8,128)S(1)}, f32[512,256]{1,0:T(8,128)S(1)}, u32[]{:S(2)}, u32[]{:S(2)}) collective-permute-start(f32[512,256]{1,0:T(8,128)S(1)} %get-tuple-element.24.away), channel_id=1, source_target_pairs={{1,2},{2,1},{3,4},{4,3},{5,6},{6,5},{7,8},{8,7},{9,10},{10,9},{11,... | collective-permute-start | bytes 1572872 | tf_op jit(solution)/shard_map/ppermute | solution.py:220
  38.0 1.9 %collective-permute-start.17 = (f32[512,256]{1,0:T(8,128)S(1)}, f32[512,256]{1,0:T(8,128)S(1)}, u32[]{:S(2)}, u32[]{:S(2)}) collective-permute-start(f32[512,256]{1,0:T(8,128)S(1)} %get-tuple-element.25.near), channel_id=1, source_target_pairs={{0,1},{1,0},{2,3},{3,2},{4,5},{5,4},{6,7},{7,6},{8,9},{9,8},{10,11... | collective-permute-start | bytes 1572872 | tf_op jit(solution)/shard_map/ppermute | solution.py:220
  39.9 0.0 copy-start.2
  39.9 1.1 %shard_map.31 = (f32[512,256]{1,0:T(8,128)S(1)}, f32[512,256]{1,0:T(8,128)S(1)}) custom-call(f32[1024,512]{1,0:T(8,128)S(1)} %copy-done.1, bf16[512,512]{1,0:T(8,128)(2,1)S(1)} %get-tuple-element.17.high, bf16[512,512]{1,0:T(8,128)(2,1)S(1)} %get-tuple-element.18.low), custom_call_target="tpu_custom_call" | custom-call | tf_op jit(solution)/shard_map/pallas_call | solution.py:263
  41.0 0.0 collective-permute-done.11.t0
  41.0 3.6 %collective-permute-start.6 = (f32[512,256]{1,0:T(8,128)S(1)}, f32[512,256]{1,0:T(8,128)S(1)}, u32[]{:S(2)}, u32[]{:S(2)}) collective-permute-start(f32[512,256]{1,0:T(8,128)S(1)} %get-tuple-element.19.away), channel_id=1, source_target_pairs={{1,2},{2,1},{3,4},{4,3},{5,6},{6,5},{7,8},{8,7},{9,10},{10,9},{11,... | collective-permute-start | bytes 1572872 | tf_op jit(solution)/shard_map/ppermute | solution.py:220
  44.7 0.0 collective-permute-done.12.t1
  44.7 1.9 %collective-permute-start.7 = (f32[512,256]{1,0:T(8,128)S(1)}, f32[512,256]{1,0:T(8,128)S(1)}, u32[]{:S(2)}, u32[]{:S(2)}) collective-permute-start(f32[512,256]{1,0:T(8,128)S(1)} %get-tuple-element.20.near), channel_id=1, source_target_pairs={{0,1},{1,0},{2,3},{3,2},{4,5},{5,4},{6,7},{7,6},{8,9},{9,8},{10,11... | collective-permute-start | bytes 1572872 | tf_op jit(solution)/shard_map/ppermute | solution.py:220
  46.6 0.5 collective-permute-done.13.t2
  47.1 0.1 shard_map.34.mine
  47.1 2.0 %collective-permute-start.14 = (f32[256,256]{1,0:T(8,128)S(1)}, f32[256,256]{1,0:T(8,128)S(1)}, u32[]{:S(2)}, u32[]{:S(2)}) collective-permute-start(f32[256,256]{1,0:T(8,128)S(1)} %shard_map.34.mine), channel_id=1, source_target_pairs={{0,1},{1,0},{2,3},{3,2},{4,5},{5,4},{6,7},{7,6},{8,9},{9,8},{10,11... | collective-permute-start | bytes 786440 | tf_op jit(solution)/shard_map/ppermute | solution.py:220
  49.1 1.5 %collective-permute-done.14.other = f32[256,256]{1,0:T(8,128)S(1)} collective-permute-done((f32[256,256]{1,0:T(8,128)S(1)}, f32[256,256]{1,0:T(8,128)S(1)}, u32[]{:S(2)}, u32[]{:S(2)}) %collective-permute-start.14) | collective-permute-done | bytes 262176 | tf_op jit(solution)/shard_map/ppermute | solution.py:220
  50.6 3.3 %shard_map.35 = (bf16[2,512,512]{2,1,0:T(8,128)(2,1)S(1)}, bf16[2,512,512]{2,1,0:T(8,128)(2,1)S(1)}) custom-call(f32[256,256]{1,0:T(8,128)S(1)} %shard_map.34.mine, f32[256,256]{1,0:T(8,128)S(1)} %collective-permute-done.14.other), custom_call_target="tpu_custom_call" | custom-call | tf_op jit(solution)/shard_map/pallas_call | solution.py:266
  53.8 7.2 %collective-permute-done.16.from_chip = f32[512,256]{1,0:T(8,128)S(1)} collective-permute-done((f32[512,256]{1,0:T(8,128)S(1)}, f32[512,256]{1,0:T(8,128)S(1)}, u32[]{:S(2)}, u32[]{:S(2)}) %collective-permute-start.16) | collective-permute-done | bytes 524320 | tf_op jit(solution)/shard_map/ppermute | solution.py:220
  61.1 0.0 collective-permute-done.17.from_core
  61.1 0.0 copy-done.2
  61.1 1.7 %shard_map.37 = (f32[256,512]{1,0:T(8,128)S(1)}, f32[256,512]{1,0:T(8,128)S(1)}) custom-call(s32[1,64]{1,0:T(1,128)S(1)} %copy-done.2, f32[512,256]{1,0:T(8,128)S(1)} %get-tuple-element.24.away, f32[512,256]{1,0:T(8,128)S(1)} %get-tuple-element.25.near, f32[512,256]{1,0:T(8,128)S(1)} %collective-permute-done.16.from_chip, ...), custom_call_target="tpu_custom_call" | custom-call | tf_op jit(solution)/shard_map/pallas_call | solution.py:279
  62.7 1.9 %collective-permute-start.18 = (f32[256,512]{1,0:T(8,128)S(1)}, f32[256,512]{1,0:T(8,128)S(1)}, u32[]{:S(2)}, u32[]{:S(2)}) collective-permute-start(f32[256,512]{1,0:T(8,128)S(1)} %get-tuple-element.26.b1), channel_id=1, source_target_pairs={{32,0},{33,1},{34,2},{35,3},{36,4},{37,5},{38,6},{39,7},{40,8},{41... | collective-permute-start | bytes 1572872 | tf_op jit(solution)/shard_map/ppermute | solution.py:220
  64.7 17.4 %collective-permute-done.6.from_chip = f32[512,256]{1,0:T(8,128)S(1)} collective-permute-done((f32[512,256]{1,0:T(8,128)S(1)}, f32[512,256]{1,0:T(8,128)S(1)}, u32[]{:S(2)}, u32[]{:S(2)}) %collective-permute-start.6) | collective-permute-done | bytes 524320 | tf_op jit(solution)/shard_map/ppermute | solution.py:220
  82.1 0.0 collective-permute-done.7.from_core
  82.1 1.7 %shard_map.36 = (f32[256,512]{1,0:T(8,128)S(1)}, f32[256,512]{1,0:T(8,128)S(1)}) custom-call(s32[1,64]{1,0:T(1,128)S(1)} %copy-done.2, f32[512,256]{1,0:T(8,128)S(1)} %get-tuple-element.19.away, f32[512,256]{1,0:T(8,128)S(1)} %get-tuple-element.20.near, f32[512,256]{1,0:T(8,128)S(1)} %collective-permute-done.6.from_chip, ...), custom_call_target="tpu_custom_call" | custom-call | tf_op jit(solution)/shard_map/pallas_call | solution.py:281
  83.8 1.9 %collective-permute-start.15 = (f32[256,512]{1,0:T(8,128)S(1)}, f32[256,512]{1,0:T(8,128)S(1)}, u32[]{:S(2)}, u32[]{:S(2)}) collective-permute-start(f32[256,512]{1,0:T(8,128)S(1)} %get-tuple-element.23.b4), channel_id=1, source_target_pairs={{0,32},{1,33},{2,34},{3,35},{4,36},{5,37},{6,38},{7,39},{8,40},{9,... | collective-permute-start | bytes 1572872 | tf_op jit(solution)/shard_map/ppermute | solution.py:220
  85.7 0.0 collective-permute-done.18.b5
  85.7 11.5 %collective-permute-done.15.b0 = f32[256,512]{1,0:T(8,128)S(1)} collective-permute-done((f32[256,512]{1,0:T(8,128)S(1)}, f32[256,512]{1,0:T(8,128)S(1)}, u32[]{:S(2)}, u32[]{:S(2)}) %collective-permute-start.15) | collective-permute-done | bytes 524320 | tf_op jit(solution)/shard_map/ppermute | solution.py:220
  97.3 1.9 %shard_map.38 = f32[1024,512]{1,0:T(8,128)} custom-call(s32[1,64]{1,0:T(1,128)S(1)} %copy-done.2, f32[256,512]{1,0:T(8,128)S(1)} %collective-permute-done.15.b0, f32[256,512]{1,0:T(8,128)S(1)} %get-tuple-element.26.b1, f32[256,512]{1,0:T(8,128)S(1)} %get-tuple-element.27.b2, f32[256,512]{1,0:T(8,128)S(1)} %get-tuple-element.28.b3, ...), custom_call_target="tpu_custom_call" | custom-call | tf_op jit(solution)/shard_map/pallas_call | solution.py:283
  (2 shorter events, 0.0 us)
Async XLA Ops:
  0.0 1.6 %copy-start = (f32[1024,512]{1,0:T(8,128)S(1)}, f32[1024,512]{1,0:T(8,128)}, u32[]{:S(2)}) copy-start(f32[1024,512]{1,0:T(8,128)} %matrix.5) | copy-start | bytes 6291460
  1.6 30.7 %copy-start.1 = (f32[1024,512]{1,0:T(8,128)S(1)}, f32[1024,512]{1,0:T(8,128)}, u32[]{:S(2)}) copy-start(f32[1024,512]{1,0:T(8,128)} %matrix.5) | copy-start | bytes 6291460
  1.6 3.6 %collective-permute-start = (f32[256,256]{1,0:T(8,128)S(1)}, f32[256,256]{1,0:T(8,128)S(1)}, u32[]{:S(2)}, u32[]{:S(2)}) collective-permute-start(f32[256,256]{1,0:T(8,128)S(1)} %shard_map.28.first.upper), channel_id=1, source_target_pairs={{0,256},{1,257},{34,290},{35,291},{68,324},{69,325},{102,358},{103... | collective-permute-start | bytes 786440 | tf_op jit(solution)/shard_map/ppermute | solution.py:220
  2.5 3.5 %collective-permute-start.1 = (f32[256,256]{1,0:T(8,128)S(1)}, f32[256,256]{1,0:T(8,128)S(1)}, u32[]{:S(2)}, u32[]{:S(2)}) collective-permute-start(f32[256,256]{1,0:T(8,128)S(1)} %shard_map.28.first.upper), channel_id=1, source_target_pairs={{0,160},{1,161},{34,130},{35,131},{68,228},{69,229},{102,198},{103... | collective-permute-start | bytes 786440 | tf_op jit(solution)/shard_map/ppermute | solution.py:220
  3.1 2.8 %collective-permute-start.2 = (f32[256,256]{1,0:T(8,128)S(1)}, f32[256,256]{1,0:T(8,128)S(1)}, u32[]{:S(2)}, u32[]{:S(2)}) collective-permute-start(f32[256,256]{1,0:T(8,128)S(1)} %shard_map.28.first.upper), channel_id=1, source_target_pairs={{0,416},{1,417},{34,386},{35,387},{68,484},{69,485},{102,454},{103... | collective-permute-start | bytes 786440 | tf_op jit(solution)/shard_map/ppermute | solution.py:220
  3.9 4.1 %collective-permute-start.10 = (f32[256,256]{1,0:T(8,128)S(1)}, f32[256,256]{1,0:T(8,128)S(1)}, u32[]{:S(2)}, u32[]{:S(2)}) collective-permute-start(f32[256,256]{1,0:T(8,128)S(1)} %shard_map.32.first), channel_id=1, source_target_pairs={{0,24},{1,25},{34,58},{35,59},{68,92},{69,93},{102,126},{103,127},... | collective-permute-start | bytes 786440 | tf_op jit(solution)/shard_map/ppermute | solution.py:220
  4.5 4.1 %collective-permute-start.8 = (f32[256,256]{1,0:T(8,128)S(1)}, f32[256,256]{1,0:T(8,128)S(1)}, u32[]{:S(2)}, u32[]{:S(2)}) collective-permute-start(f32[256,256]{1,0:T(8,128)S(1)} %shard_map.32.first), channel_id=1, source_target_pairs={{0,16},{1,17},{34,50},{35,51},{68,84},{69,85},{102,118},{103,119},... | collective-permute-start | bytes 786440 | tf_op jit(solution)/shard_map/ppermute | solution.py:220
  5.2 3.5 %collective-permute-start.9 = (f32[256,256]{1,0:T(8,128)S(1)}, f32[256,256]{1,0:T(8,128)S(1)}, u32[]{:S(2)}, u32[]{:S(2)}) collective-permute-start(f32[256,256]{1,0:T(8,128)S(1)} %shard_map.32.first), channel_id=1, source_target_pairs={{0,8},{1,9},{34,42},{35,43},{68,76},{69,77},{102,110},{103,111},{1... | collective-permute-start | bytes 786440 | tf_op jit(solution)/shard_map/ppermute | solution.py:220
  6.0 4.1 %collective-permute-start.3 = (f32[256,256]{1,0:T(8,128)S(1)}, f32[256,256]{1,0:T(8,128)S(1)}, u32[]{:S(2)}, u32[]{:S(2)}) collective-permute-start(f32[256,256]{1,0:T(8,128)S(1)} %shard_map.29.t0), channel_id=1, source_target_pairs={{0,32},{256,288},{160,128},{416,384},{1,33},{257,289},{161,129},{4... | collective-permute-start | bytes 786440 | tf_op jit(solution)/shard_map/ppermute | solution.py:220
  6.7 25.7 %collective-permute-start.4 = (f32[256,256]{1,0:T(8,128)S(1)}, f32[256,256]{1,0:T(8,128)S(1)}, u32[]{:S(2)}, u32[]{:S(2)}) collective-permute-start(f32[256,256]{1,0:T(8,128)S(1)} %shard_map.29.t0), channel_id=1, source_target_pairs={{0,64},{256,320},{160,224},{416,480},{1,65},{257,321},{161,225},{4... | collective-permute-start | bytes 786440 | tf_op jit(solution)/shard_map/ppermute | solution.py:220
  8.0 24.4 %collective-permute-start.5 = (f32[256,256]{1,0:T(8,128)S(1)}, f32[256,256]{1,0:T(8,128)S(1)}, u32[]{:S(2)}, u32[]{:S(2)}) collective-permute-start(f32[256,256]{1,0:T(8,128)S(1)} %shard_map.29.t0), channel_id=1, source_target_pairs={{0,448},{256,192},{160,96},{416,352},{1,449},{257,193},{161,97},{4... | collective-permute-start | bytes 786440 | tf_op jit(solution)/shard_map/ppermute | solution.py:220
  8.8 32.2 %collective-permute-start.11 = (f32[256,256]{1,0:T(8,128)S(1)}, f32[256,256]{1,0:T(8,128)S(1)}, u32[]{:S(2)}, u32[]{:S(2)}) collective-permute-start(f32[256,256]{1,0:T(8,128)S(1)} %shard_map.33.first), channel_id=1, source_target_pairs={{0,4},{16,20},{8,12},{24,28},{1,5},{17,21},{9,13},{25,29},{34,38},... | collective-permute-start | bytes 786440 | tf_op jit(solution)/shard_map/ppermute | solution.py:220
  9.5 35.2 %collective-permute-start.12 = (f32[256,256]{1,0:T(8,128)S(1)}, f32[256,256]{1,0:T(8,128)S(1)}, u32[]{:S(2)}, u32[]{:S(2)}) collective-permute-start(f32[256,256]{1,0:T(8,128)S(1)} %shard_map.33.first), channel_id=1, source_target_pairs={{0,2},{16,18},{8,10},{24,26},{1,3},{17,19},{9,11},{25,27},{34,32},... | collective-permute-start | bytes 786440 | tf_op jit(solution)/shard_map/ppermute | solution.py:220
  10.1 36.9 %collective-permute-start.13 = (f32[256,256]{1,0:T(8,128)S(1)}, f32[256,256]{1,0:T(8,128)S(1)}, u32[]{:S(2)}, u32[]{:S(2)}) collective-permute-start(f32[256,256]{1,0:T(8,128)S(1)} %shard_map.33.first), channel_id=1, source_target_pairs={{0,6},{16,22},{8,14},{24,30},{1,7},{17,23},{9,15},{25,31},{34,36},... | collective-permute-start | bytes 786440 | tf_op jit(solution)/shard_map/ppermute | solution.py:220
  36.1 25.0 %collective-permute-start.16 = (f32[512,256]{1,0:T(8,128)S(1)}, f32[512,256]{1,0:T(8,128)S(1)}, u32[]{:S(2)}, u32[]{:S(2)}) collective-permute-start(f32[512,256]{1,0:T(8,128)S(1)} %get-tuple-element.24.away), channel_id=1, source_target_pairs={{1,2},{2,1},{3,4},{4,3},{5,6},{6,5},{7,8},{8,7},{9,10},{10,9},{11,... | collective-permute-start | bytes 1572872 | tf_op jit(solution)/shard_map/ppermute | solution.py:220
  38.0 23.1 %collective-permute-start.17 = (f32[512,256]{1,0:T(8,128)S(1)}, f32[512,256]{1,0:T(8,128)S(1)}, u32[]{:S(2)}, u32[]{:S(2)}) collective-permute-start(f32[512,256]{1,0:T(8,128)S(1)} %get-tuple-element.25.near), channel_id=1, source_target_pairs={{0,1},{1,0},{2,3},{3,2},{4,5},{5,4},{6,7},{7,6},{8,9},{9,8},{10,11... | collective-permute-start | bytes 1572872 | tf_op jit(solution)/shard_map/ppermute | solution.py:220
  39.9 21.1 %copy-start.2 = (s32[1,64]{1,0:T(1,128)S(1)}, s32[1,64]{1,0:T(1,128)}, u32[]{:S(2)}) copy-start(s32[1,64]{1,0:T(1,128)} %moves.5) | copy-start | bytes 772
  41.0 41.1 %collective-permute-start.6 = (f32[512,256]{1,0:T(8,128)S(1)}, f32[512,256]{1,0:T(8,128)S(1)}, u32[]{:S(2)}, u32[]{:S(2)}) collective-permute-start(f32[512,256]{1,0:T(8,128)S(1)} %get-tuple-element.19.away), channel_id=1, source_target_pairs={{1,2},{2,1},{3,4},{4,3},{5,6},{6,5},{7,8},{8,7},{9,10},{10,9},{11,... | collective-permute-start | bytes 1572872 | tf_op jit(solution)/shard_map/ppermute | solution.py:220
  44.7 37.4 %collective-permute-start.7 = (f32[512,256]{1,0:T(8,128)S(1)}, f32[512,256]{1,0:T(8,128)S(1)}, u32[]{:S(2)}, u32[]{:S(2)}) collective-permute-start(f32[512,256]{1,0:T(8,128)S(1)} %get-tuple-element.20.near), channel_id=1, source_target_pairs={{0,1},{1,0},{2,3},{3,2},{4,5},{5,4},{6,7},{7,6},{8,9},{9,8},{10,11... | collective-permute-start | bytes 1572872 | tf_op jit(solution)/shard_map/ppermute | solution.py:220
  47.1 3.4 %collective-permute-start.14 = (f32[256,256]{1,0:T(8,128)S(1)}, f32[256,256]{1,0:T(8,128)S(1)}, u32[]{:S(2)}, u32[]{:S(2)}) collective-permute-start(f32[256,256]{1,0:T(8,128)S(1)} %shard_map.34.mine), channel_id=1, source_target_pairs={{0,1},{1,0},{2,3},{3,2},{4,5},{5,4},{6,7},{7,6},{8,9},{9,8},{10,11... | collective-permute-start | bytes 786440 | tf_op jit(solution)/shard_map/ppermute | solution.py:220
  62.7 23.0 %collective-permute-start.18 = (f32[256,512]{1,0:T(8,128)S(1)}, f32[256,512]{1,0:T(8,128)S(1)}, u32[]{:S(2)}, u32[]{:S(2)}) collective-permute-start(f32[256,512]{1,0:T(8,128)S(1)} %get-tuple-element.26.b1), channel_id=1, source_target_pairs={{32,0},{33,1},{34,2},{35,3},{36,4},{37,5},{38,6},{39,7},{40,8},{41... | collective-permute-start | bytes 1572872 | tf_op jit(solution)/shard_map/ppermute | solution.py:220
  83.8 13.5 %collective-permute-start.15 = (f32[256,512]{1,0:T(8,128)S(1)}, f32[256,512]{1,0:T(8,128)S(1)}, u32[]{:S(2)}, u32[]{:S(2)}) collective-permute-start(f32[256,512]{1,0:T(8,128)S(1)} %get-tuple-element.23.b4), channel_id=1, source_target_pairs={{0,32},{1,33},{2,34},{3,35},{4,36},{5,37},{6,38},{7,39},{8,40},{9,... | collective-permute-start | bytes 1572872 | tf_op jit(solution)/shard_map/ppermute | solution.py:220

commit v4 on v3

--- a/solution.py
+++ b/solution.py
@@ -65,13 +65,6 @@
     return results
 
 
-def pivot_kernel(matrix, upper, loaded):
-    first = pl.multiple_of(lax.axis_index("col") % 2 * SPAN, SPAN)
-    load = pltpu.make_async_copy(matrix.at[pl.ds(first, BLOCK), pl.ds(BLOCK, BLOCK)], upper, loaded)
-    load.start()
-    load.wait()
-
-
 def again_kernel(upper, copy):
     copy[...] = upper[...]
 
@@ -143,12 +136,12 @@
     lower[...] = turned[BLOCK:]
 
 
-def place_kernel(moves, b0, b1, b2, b3, b4, b5, result, stored):
+def place_blocks(offsets, moves, blocks, result, stored):
     r = lax.axis_index("row")
 
     def copies(act):
-        for number, block in enumerate((b0, b1, b2, b3, b4, b5)):
-            slot = 4 * r - 1 + number
+        for number, (offset, block) in enumerate(zip(offsets, blocks)):
+            slot = 4 * r + offset
             known = (slot >= 0) & (slot < moves.shape[1])
             target = moves[0, jnp.clip(slot, 0, moves.shape[1] - 1)] - 4 * r
 
@@ -161,6 +154,15 @@
     copies(lambda copy: copy.wait())
 
 
+def own_kernel(moves, b0, b1, b2, b3, result, stored):
+    place_blocks((0, 1, 2, 3), moves, (b0, b1, b2, b3), result, stored)
+
+
+def arrivals_kernel(moves, above, below, partial, result, stored):
+    del partial
+    place_blocks((-1, 4), moves, (above, below), result, stored)
+
+
 SMEM = pl.BlockSpec(memory_space=pltpu.SMEM)
 VMEM = pl.BlockSpec(memory_space=pltpu.VMEM)
 HBM = pl.BlockSpec(memory_space=pltpu.HBM)
@@ -174,13 +176,14 @@
     return jax.ShapeDtypeStruct(shape, jnp.bfloat16)
 
 
-def call(kernel, out_shape, in_specs, out_specs, scratch, products):
+def call(kernel, out_shape, in_specs, out_specs, scratch, products, aliases=None):
     return pl.pallas_call(
         kernel,
         out_shape=out_shape,
         in_specs=in_specs,
         out_specs=out_specs,
         scratch_shapes=scratch,
+        input_output_aliases=aliases or {},
         cost_estimate=pl.CostEstimate(
             flops=products * 3 * 2 * BLOCK**3, bytes_accessed=0, transcendentals=0
         ),
@@ -236,9 +239,8 @@
 
 
 def body(matrix, moves):
-    upper = call(
-        pivot_kernel, f32(BLOCK, BLOCK), [HBM], VMEM, [pltpu.SemaphoreType.DMA(())], 0
-    )(matrix)
+    odd = lax.axis_index("col") % 2
+    upper = lax.dynamic_slice(matrix, (odd * SPAN, BLOCK), (BLOCK, BLOCK))
     again = call(again_kernel, f32(BLOCK, BLOCK), [VMEM], VMEM, [], 0)(upper)
     join = call(join_kernel, f32(BLOCK, BLOCK), [VMEM] * 4, VMEM, [], 0)
     col_token = join(upper, *[send(upper, pairs) for pairs in ROWS_1])
@@ -280,9 +282,18 @@
     below = send(first, UP)
     third, fourth = turn[1](moves, *parts[1], high, low)
     above = send(fourth, DOWN)
+    partial = call(
+        own_kernel, f32(*matrix.shape), [SMEM] + [VMEM] * 4, HBM, [pltpu.SemaphoreType.DMA((4,))], 0
+    )(moves, first, second, third, fourth)
     return call(
-        place_kernel, f32(*matrix.shape), [SMEM] + [VMEM] * 6, HBM, [pltpu.SemaphoreType.DMA((6,))], 0
-    )(moves, above, first, second, third, fourth, below)
+        arrivals_kernel,
+        f32(*matrix.shape),
+        [SMEM] + [VMEM] * 2 + [HBM],
+        HBM,
+        [pltpu.SemaphoreType.DMA((2,))],
+        0,
+        aliases={3: 0},
+    )(moves, above, below, partial)
 
 
 def solution(mesh):

time: 99.7 us -> 98.6 us (0.989)
  waiting for transfers between devices: 59 us -> 57.3 us
  Pallas kernels: 13.5 us -> 14.7 us
    ppermute x19, waiting for transfers between devices: 59 us -> 57.3 us  [send(): return lax.ppermute(x, AXES, pairs)]
    unnamed x6 -> x4, local copies, waits for them, and re-layouts: 1.6 us -> 0.01 us
    pallas_call x2, Pallas kernels: 1.96 us -> 3.11 us  [the longest x1 1.74 us: body(): call(own_kernel, f32(*matrix.shape), [SMEM] + [VMEM] * 4, HBM, [pltpu.Sem...]
    dynamic_slice x0 -> x1, local copies, waits for them, and re-layouts: none -> 1.12 us  [body(): upper = lax.dynamic_slice(matrix, (odd * SPAN, BLOCK), (BLOCK, BLOCK))]
  transfers between devices with their start and end apart: 19 -> 19, of which waited for: 6 -> 6; matrix products, arithmetic and copies ran while one was open for 0% -> 0% of each run, Pallas kernels for 12% -> 14%
where the time goes in v4:
time: 98.6 us; the launch traced here: 98 us
  waiting for transfers between devices  57.3 us (58%)
  starting transfers between devices  24.6 us (25%)
  Pallas kernels  14.7 us (15%)
  local copies, waits for them, and re-layouts  1.13 us (1%)
    ppermute x19, waiting for transfers between devices, send(): return lax.ppermute(x, AXES, pairs)  57.3 us
    ppermute x19, starting transfers between devices, send(): return lax.ppermute(x, AXES, pairs)  24.6 us
    pallas_call x1, Pallas kernels, body(): call(first_columns_kernel, (half, half, bf16(SPAN, SPAN), bf16(SPAN, SPAN...  3.7 us
    pallas_call x1, Pallas kernels, body(): call(rotations_kernel, (bf16(2, SPAN, SPAN),) * 2, [VMEM] * 2, (VMEM,) *...  3.28 us
  transfers between devices with their start and end apart: 19, of which 6 were waited for; matrix products, arithmetic and copies ran while one was open for 0% of the time, Pallas kernels for 14%

profile of v4, /device:TPU:194, one launch (start us, length us, event | category | flops | bytes accessed | tf_op | source)
XLA Modules:
  0.0 98.0 jit_solution(12153578483193004726)
XLA Ops:
  0.0 0.0 copy-start
  0.0 1.1 %constant_dynamic-slice_fusion.first.upper = f32[256,256]{1,0:T(8,128)S(1)} fusion(f32[1024,512]{1,0:T(8,128)} %matrix.3, s32[]{:T(128)S(6)} %select_n.11), kind=kLoop, calls=%fused_computation | loop fusion | bytes 524292 | tf_op jit(solution)/shard_map/dynamic_slice | solution.py:243
  1.1 0.7 collective-permute-start
  1.8 0.7 collective-permute-start.1
  2.5 0.7 collective-permute-start.2
  3.2 0.7 collective-permute-start.10
  3.9 0.7 collective-permute-start.8
  4.6 0.0 collective-permute-done.t0
  4.6 0.7 collective-permute-start.9
  5.3 0.0 collective-permute-done.1.t1
  5.3 0.0 collective-permute-done.2.t2
  5.3 0.1 shard_map.28.t0
  5.4 0.7 collective-permute-start.3
  6.0 1.3 %collective-permute-start.4 = (f32[256,256]{1,0:T(8,128)S(1)}, f32[256,256]{1,0:T(8,128)S(1)}, u32[]{:S(2)}, u32[]{:S(2)}) collective-permute-start(f32[256,256]{1,0:T(8,128)S(1)} %shard_map.28.t0), channel_id=1, source_target_pairs={{0,64},{256,320},{160,224},{416,480},{1,65},{257,321},{161,225},{4... | collective-permute-start | bytes 786440 | tf_op jit(solution)/shard_map/ppermute | solution.py:223
  7.3 0.0 collective-permute-done.10.t2
  7.3 0.7 collective-permute-start.5
  8.0 0.0 collective-permute-done.8.t0
  8.0 0.0 collective-permute-done.9.t1
  8.1 0.1 shard_map.32.first
  8.1 0.7 collective-permute-start.11
  8.8 0.7 collective-permute-start.12
  9.5 0.0 collective-permute-done.3.t1
  9.5 1.3 %collective-permute-start.13 = (f32[256,256]{1,0:T(8,128)S(1)}, f32[256,256]{1,0:T(8,128)S(1)}, u32[]{:S(2)}, u32[]{:S(2)}) collective-permute-start(f32[256,256]{1,0:T(8,128)S(1)} %shard_map.32.first), channel_id=1, source_target_pairs={{0,6},{16,22},{8,14},{24,30},{1,7},{17,23},{9,15},{25,31},{34,36},... | collective-permute-start | bytes 786440 | tf_op jit(solution)/shard_map/ppermute | solution.py:223
  10.8 20.9 %collective-permute-done.4.t2 = f32[256,256]{1,0:T(8,128)S(1)} collective-permute-done((f32[256,256]{1,0:T(8,128)S(1)}, f32[256,256]{1,0:T(8,128)S(1)}, u32[]{:S(2)}, u32[]{:S(2)}) %collective-permute-start.4) | collective-permute-done | bytes 262176 | tf_op jit(solution)/shard_map/ppermute | solution.py:223
  31.7 0.0 collective-permute-done.5.t3
  31.7 0.0 copy-done
  31.7 3.7 %shard_map.29 = (f32[512,256]{1,0:T(8,128)S(1)}, f32[512,256]{1,0:T(8,128)S(1)}, bf16[512,512]{1,0:T(8,128)(2,1)S(1)}, bf16[512,512]{1,0:T(8,128)(2,1)S(1)}) custom-call(f32[1024,512]{1,0:T(8,128)S(1)} %copy-done, f32[256,256]{1,0:T(8,128)S(1)} %shard_map.28.t0, f32[256,256]{1,0:T(8,128)S(1)} %collective-permute-done.3.t1, ...), custom_call_target="tpu_custom_call" | custom-call | tf_op jit(solution)/shard_map/pallas_call | solution.py:256
  35.4 1.9 %collective-permute-start.16 = (f32[512,256]{1,0:T(8,128)S(1)}, f32[512,256]{1,0:T(8,128)S(1)}, u32[]{:S(2)}, u32[]{:S(2)}) collective-permute-start(f32[512,256]{1,0:T(8,128)S(1)} %get-tuple-element.24.away), channel_id=1, source_target_pairs={{1,2},{2,1},{3,4},{4,3},{5,6},{6,5},{7,8},{8,7},{9,10},{10,9},{11,... | collective-permute-start | bytes 1572872 | tf_op jit(solution)/shard_map/ppermute | solution.py:223
  37.3 1.9 %collective-permute-start.17 = (f32[512,256]{1,0:T(8,128)S(1)}, f32[512,256]{1,0:T(8,128)S(1)}, u32[]{:S(2)}, u32[]{:S(2)}) collective-permute-start(f32[512,256]{1,0:T(8,128)S(1)} %get-tuple-element.25.near), channel_id=1, source_target_pairs={{0,1},{1,0},{2,3},{3,2},{4,5},{5,4},{6,7},{7,6},{8,9},{9,8},{10,11... | collective-permute-start | bytes 1572872 | tf_op jit(solution)/shard_map/ppermute | solution.py:223
  39.3 0.0 copy-start.1
  39.3 1.1 %shard_map.30 = (f32[512,256]{1,0:T(8,128)S(1)}, f32[512,256]{1,0:T(8,128)S(1)}) custom-call(f32[1024,512]{1,0:T(8,128)S(1)} %copy-done, bf16[512,512]{1,0:T(8,128)(2,1)S(1)} %get-tuple-element.17.high, bf16[512,512]{1,0:T(8,128)(2,1)S(1)} %get-tuple-element.18.low), custom_call_target="tpu_custom_call" | custom-call | tf_op jit(solution)/shard_map/pallas_call | solution.py:265
  40.4 0.0 collective-permute-done.11.t0
  40.4 3.6 %collective-permute-start.6 = (f32[512,256]{1,0:T(8,128)S(1)}, f32[512,256]{1,0:T(8,128)S(1)}, u32[]{:S(2)}, u32[]{:S(2)}) collective-permute-start(f32[512,256]{1,0:T(8,128)S(1)} %get-tuple-element.19.away), channel_id=1, source_target_pairs={{1,2},{2,1},{3,4},{4,3},{5,6},{6,5},{7,8},{8,7},{9,10},{10,9},{11,... | collective-permute-start | bytes 1572872 | tf_op jit(solution)/shard_map/ppermute | solution.py:223
  44.0 0.0 collective-permute-done.12.t1
  44.0 1.9 %collective-permute-start.7 = (f32[512,256]{1,0:T(8,128)S(1)}, f32[512,256]{1,0:T(8,128)S(1)}, u32[]{:S(2)}, u32[]{:S(2)}) collective-permute-start(f32[512,256]{1,0:T(8,128)S(1)} %get-tuple-element.20.near), channel_id=1, source_target_pairs={{0,1},{1,0},{2,3},{3,2},{4,5},{5,4},{6,7},{7,6},{8,9},{9,8},{10,11... | collective-permute-start | bytes 1572872 | tf_op jit(solution)/shard_map/ppermute | solution.py:223
  46.0 0.5 collective-permute-done.13.t2
  46.4 0.1 shard_map.33.mine
  46.5 2.0 %collective-permute-start.14 = (f32[256,256]{1,0:T(8,128)S(1)}, f32[256,256]{1,0:T(8,128)S(1)}, u32[]{:S(2)}, u32[]{:S(2)}) collective-permute-start(f32[256,256]{1,0:T(8,128)S(1)} %shard_map.33.mine), channel_id=1, source_target_pairs={{0,1},{1,0},{2,3},{3,2},{4,5},{5,4},{6,7},{7,6},{8,9},{9,8},{10,11... | collective-permute-start | bytes 786440 | tf_op jit(solution)/shard_map/ppermute | solution.py:223
  48.4 1.5 %collective-permute-done.14.other = f32[256,256]{1,0:T(8,128)S(1)} collective-permute-done((f32[256,256]{1,0:T(8,128)S(1)}, f32[256,256]{1,0:T(8,128)S(1)}, u32[]{:S(2)}, u32[]{:S(2)}) %collective-permute-start.14) | collective-permute-done | bytes 262176 | tf_op jit(solution)/shard_map/ppermute | solution.py:223
  49.9 3.3 %shard_map.34 = (bf16[2,512,512]{2,1,0:T(8,128)(2,1)S(1)}, bf16[2,512,512]{2,1,0:T(8,128)(2,1)S(1)}) custom-call(f32[256,256]{1,0:T(8,128)S(1)} %shard_map.33.mine, f32[256,256]{1,0:T(8,128)S(1)} %collective-permute-done.14.other), custom_call_target="tpu_custom_call" | custom-call | tf_op jit(solution)/shard_map/pallas_call | solution.py:268
  53.2 7.2 %collective-permute-done.16.from_chip = f32[512,256]{1,0:T(8,128)S(1)} collective-permute-done((f32[512,256]{1,0:T(8,128)S(1)}, f32[512,256]{1,0:T(8,128)S(1)}, u32[]{:S(2)}, u32[]{:S(2)}) %collective-permute-start.16) | collective-permute-done | bytes 524320 | tf_op jit(solution)/shard_map/ppermute | solution.py:223
  60.4 0.0 collective-permute-done.17.from_core
  60.4 0.0 copy-done.1
  60.4 1.7 %shard_map.36 = (f32[256,512]{1,0:T(8,128)S(1)}, f32[256,512]{1,0:T(8,128)S(1)}) custom-call(s32[1,64]{1,0:T(1,128)S(1)} %copy-done.1, f32[512,256]{1,0:T(8,128)S(1)} %get-tuple-element.24.away, f32[512,256]{1,0:T(8,128)S(1)} %get-tuple-element.25.near, f32[512,256]{1,0:T(8,128)S(1)} %collective-permute-done.16.from_chip, ...), custom_call_target="tpu_custom_call" | custom-call | tf_op jit(solution)/shard_map/pallas_call | solution.py:281
  62.1 1.9 %collective-permute-start.18 = (f32[256,512]{1,0:T(8,128)S(1)}, f32[256,512]{1,0:T(8,128)S(1)}, u32[]{:S(2)}, u32[]{:S(2)}) collective-permute-start(f32[256,512]{1,0:T(8,128)S(1)} %get-tuple-element.26.b0), channel_id=1, source_target_pairs={{32,0},{33,1},{34,2},{35,3},{36,4},{37,5},{38,6},{39,7},{40,8},{41... | collective-permute-start | bytes 1572872 | tf_op jit(solution)/shard_map/ppermute | solution.py:223
  64.0 17.4 %collective-permute-done.6.from_chip = f32[512,256]{1,0:T(8,128)S(1)} collective-permute-done((f32[512,256]{1,0:T(8,128)S(1)}, f32[512,256]{1,0:T(8,128)S(1)}, u32[]{:S(2)}, u32[]{:S(2)}) %collective-permute-start.6) | collective-permute-done | bytes 524320 | tf_op jit(solution)/shard_map/ppermute | solution.py:223
  81.4 0.0 collective-permute-done.7.from_core
  81.4 1.7 %shard_map.35 = (f32[256,512]{1,0:T(8,128)S(1)}, f32[256,512]{1,0:T(8,128)S(1)}) custom-call(s32[1,64]{1,0:T(1,128)S(1)} %copy-done.1, f32[512,256]{1,0:T(8,128)S(1)} %get-tuple-element.19.away, f32[512,256]{1,0:T(8,128)S(1)} %get-tuple-element.20.near, f32[512,256]{1,0:T(8,128)S(1)} %collective-permute-done.6.from_chip, ...), custom_call_target="tpu_custom_call" | custom-call | tf_op jit(solution)/shard_map/pallas_call | solution.py:283
  83.1 1.9 %collective-permute-start.15 = (f32[256,512]{1,0:T(8,128)S(1)}, f32[256,512]{1,0:T(8,128)S(1)}, u32[]{:S(2)}, u32[]{:S(2)}) collective-permute-start(f32[256,512]{1,0:T(8,128)S(1)} %get-tuple-element.23.b3), channel_id=1, source_target_pairs={{0,32},{1,33},{2,34},{3,35},{4,36},{5,37},{6,38},{7,39},{8,40},{9,... | collective-permute-start | bytes 1572872 | tf_op jit(solution)/shard_map/ppermute | solution.py:223
  85.0 1.7 %shard_map.37.partial = f32[1024,512]{1,0:T(8,128)} custom-call(s32[1,64]{1,0:T(1,128)S(1)} %copy-done.1, f32[256,512]{1,0:T(8,128)S(1)} %get-tuple-element.26.b0, f32[256,512]{1,0:T(8,128)S(1)} %get-tuple-element.27.b1, f32[256,512]{1,0:T(8,128)S(1)} %get-tuple-element.28.b2, f32[256,512]{1,0:T(8,128)S(1)} %get-tuple-element.23.b3), custom_call_target="tpu_custom_call" | custom-call | tf_op jit(solution)/shard_map/pallas_call | solution.py:285
  86.8 0.0 collective-permute-done.18.below
  86.8 9.8 %collective-permute-done.15.above = f32[256,512]{1,0:T(8,128)S(1)} collective-permute-done((f32[256,512]{1,0:T(8,128)S(1)}, f32[256,512]{1,0:T(8,128)S(1)}, u32[]{:S(2)}, u32[]{:S(2)}) %collective-permute-start.15) | collective-permute-done | bytes 524320 | tf_op jit(solution)/shard_map/ppermute | solution.py:223
  96.6 1.4 %shard_map.38 = f32[1024,512]{1,0:T(8,128)} custom-call(s32[1,64]{1,0:T(1,128)S(1)} %copy-done.1, f32[256,512]{1,0:T(8,128)S(1)} %collective-permute-done.15.above, f32[256,512]{1,0:T(8,128)S(1)} %collective-permute-done.18.below, f32[1024,512]{1,0:T(8,128)} %shard_map.37.partial), custom_call_target="tpu_custom_call", output_to_operand_aliasing={{}: (3, {})} | custom-call | tf_op jit(solution)/shard_map/pallas_call | solution.py:288
  (1 shorter events, 0.0 us)
Async XLA Ops:
  0.0 31.7 %copy-start = (f32[1024,512]{1,0:T(8,128)S(1)}, f32[1024,512]{1,0:T(8,128)}, u32[]{:S(2)}) copy-start(f32[1024,512]{1,0:T(8,128)} %matrix.3) | copy-start | bytes 6291460
  1.1 3.5 %collective-permute-start = (f32[256,256]{1,0:T(8,128)S(1)}, f32[256,256]{1,0:T(8,128)S(1)}, u32[]{:S(2)}, u32[]{:S(2)}) collective-permute-start(f32[256,256]{1,0:T(8,128)S(1)} %constant_dynamic-slice_fusion.first.upper), channel_id=1, source_target_pairs={{0,256},{1,257},{34,290},{35,291},{68,324},{69,325},{102,358},{103... | collective-permute-start | bytes 786440 | tf_op jit(solution)/shard_map/ppermute | solution.py:223
  1.8 3.5 %collective-permute-start.1 = (f32[256,256]{1,0:T(8,128)S(1)}, f32[256,256]{1,0:T(8,128)S(1)}, u32[]{:S(2)}, u32[]{:S(2)}) collective-permute-start(f32[256,256]{1,0:T(8,128)S(1)} %constant_dynamic-slice_fusion.first.upper), channel_id=1, source_target_pairs={{0,160},{1,161},{34,130},{35,131},{68,228},{69,229},{102,198},{103... | collective-permute-start | bytes 786440 | tf_op jit(solution)/shard_map/ppermute | solution.py:223
  2.5 2.8 %collective-permute-start.2 = (f32[256,256]{1,0:T(8,128)S(1)}, f32[256,256]{1,0:T(8,128)S(1)}, u32[]{:S(2)}, u32[]{:S(2)}) collective-permute-start(f32[256,256]{1,0:T(8,128)S(1)} %constant_dynamic-slice_fusion.first.upper), channel_id=1, source_target_pairs={{0,416},{1,417},{34,386},{35,387},{68,484},{69,485},{102,454},{103... | collective-permute-start | bytes 786440 | tf_op jit(solution)/shard_map/ppermute | solution.py:223
  3.2 4.1 %collective-permute-start.10 = (f32[256,256]{1,0:T(8,128)S(1)}, f32[256,256]{1,0:T(8,128)S(1)}, u32[]{:S(2)}, u32[]{:S(2)}) collective-permute-start(f32[256,256]{1,0:T(8,128)S(1)} %shard_map.31.first), channel_id=1, source_target_pairs={{0,24},{1,25},{34,58},{35,59},{68,92},{69,93},{102,126},{103,127},... | collective-permute-start | bytes 786440 | tf_op jit(solution)/shard_map/ppermute | solution.py:223
  3.9 4.1 %collective-permute-start.8 = (f32[256,256]{1,0:T(8,128)S(1)}, f32[256,256]{1,0:T(8,128)S(1)}, u32[]{:S(2)}, u32[]{:S(2)}) collective-permute-start(f32[256,256]{1,0:T(8,128)S(1)} %shard_map.31.first), channel_id=1, source_target_pairs={{0,16},{1,17},{34,50},{35,51},{68,84},{69,85},{102,118},{103,119},... | collective-permute-start | bytes 786440 | tf_op jit(solution)/shard_map/ppermute | solution.py:223
  4.6 3.5 %collective-permute-start.9 = (f32[256,256]{1,0:T(8,128)S(1)}, f32[256,256]{1,0:T(8,128)S(1)}, u32[]{:S(2)}, u32[]{:S(2)}) collective-permute-start(f32[256,256]{1,0:T(8,128)S(1)} %shard_map.31.first), channel_id=1, source_target_pairs={{0,8},{1,9},{34,42},{35,43},{68,76},{69,77},{102,110},{103,111},{1... | collective-permute-start | bytes 786440 | tf_op jit(solution)/shard_map/ppermute | solution.py:223
  5.4 4.1 %collective-permute-start.3 = (f32[256,256]{1,0:T(8,128)S(1)}, f32[256,256]{1,0:T(8,128)S(1)}, u32[]{:S(2)}, u32[]{:S(2)}) collective-permute-start(f32[256,256]{1,0:T(8,128)S(1)} %shard_map.28.t0), channel_id=1, source_target_pairs={{0,32},{256,288},{160,128},{416,384},{1,33},{257,289},{161,129},{4... | collective-permute-start | bytes 786440 | tf_op jit(solution)/shard_map/ppermute | solution.py:223
  6.0 25.7 %collective-permute-start.4 = (f32[256,256]{1,0:T(8,128)S(1)}, f32[256,256]{1,0:T(8,128)S(1)}, u32[]{:S(2)}, u32[]{:S(2)}) collective-permute-start(f32[256,256]{1,0:T(8,128)S(1)} %shard_map.28.t0), channel_id=1, source_target_pairs={{0,64},{256,320},{160,224},{416,480},{1,65},{257,321},{161,225},{4... | collective-permute-start | bytes 786440 | tf_op jit(solution)/shard_map/ppermute | solution.py:223
  7.3 24.4 %collective-permute-start.5 = (f32[256,256]{1,0:T(8,128)S(1)}, f32[256,256]{1,0:T(8,128)S(1)}, u32[]{:S(2)}, u32[]{:S(2)}) collective-permute-start(f32[256,256]{1,0:T(8,128)S(1)} %shard_map.28.t0), channel_id=1, source_target_pairs={{0,448},{256,192},{160,96},{416,352},{1,449},{257,193},{161,97},{4... | collective-permute-start | bytes 786440 | tf_op jit(solution)/shard_map/ppermute | solution.py:223
  8.1 32.2 %collective-permute-start.11 = (f32[256,256]{1,0:T(8,128)S(1)}, f32[256,256]{1,0:T(8,128)S(1)}, u32[]{:S(2)}, u32[]{:S(2)}) collective-permute-start(f32[256,256]{1,0:T(8,128)S(1)} %shard_map.32.first), channel_id=1, source_target_pairs={{0,4},{16,20},{8,12},{24,28},{1,5},{17,21},{9,13},{25,29},{34,38},... | collective-permute-start | bytes 786440 | tf_op jit(solution)/shard_map/ppermute | solution.py:223
  8.8 35.2 %collective-permute-start.12 = (f32[256,256]{1,0:T(8,128)S(1)}, f32[256,256]{1,0:T(8,128)S(1)}, u32[]{:S(2)}, u32[]{:S(2)}) collective-permute-start(f32[256,256]{1,0:T(8,128)S(1)} %shard_map.32.first), channel_id=1, source_target_pairs={{0,2},{16,18},{8,10},{24,26},{1,3},{17,19},{9,11},{25,27},{34,32},... | collective-permute-start | bytes 786440 | tf_op jit(solution)/shard_map/ppermute | solution.py:223
  9.5 36.9 %collective-permute-start.13 = (f32[256,256]{1,0:T(8,128)S(1)}, f32[256,256]{1,0:T(8,128)S(1)}, u32[]{:S(2)}, u32[]{:S(2)}) collective-permute-start(f32[256,256]{1,0:T(8,128)S(1)} %shard_map.32.first), channel_id=1, source_target_pairs={{0,6},{16,22},{8,14},{24,30},{1,7},{17,23},{9,15},{25,31},{34,36},... | collective-permute-start | bytes 786440 | tf_op jit(solution)/shard_map/ppermute | solution.py:223
  35.4 25.0 %collective-permute-start.16 = (f32[512,256]{1,0:T(8,128)S(1)}, f32[512,256]{1,0:T(8,128)S(1)}, u32[]{:S(2)}, u32[]{:S(2)}) collective-permute-start(f32[512,256]{1,0:T(8,128)S(1)} %get-tuple-element.24.away), channel_id=1, source_target_pairs={{1,2},{2,1},{3,4},{4,3},{5,6},{6,5},{7,8},{8,7},{9,10},{10,9},{11,... | collective-permute-start | bytes 1572872 | tf_op jit(solution)/shard_map/ppermute | solution.py:223
  37.3 23.1 %collective-permute-start.17 = (f32[512,256]{1,0:T(8,128)S(1)}, f32[512,256]{1,0:T(8,128)S(1)}, u32[]{:S(2)}, u32[]{:S(2)}) collective-permute-start(f32[512,256]{1,0:T(8,128)S(1)} %get-tuple-element.25.near), channel_id=1, source_target_pairs={{0,1},{1,0},{2,3},{3,2},{4,5},{5,4},{6,7},{7,6},{8,9},{9,8},{10,11... | collective-permute-start | bytes 1572872 | tf_op jit(solution)/shard_map/ppermute | solution.py:223
  39.3 21.1 %copy-start.1 = (s32[1,64]{1,0:T(1,128)S(1)}, s32[1,64]{1,0:T(1,128)}, u32[]{:S(2)}) copy-start(s32[1,64]{1,0:T(1,128)} %moves.7) | copy-start | bytes 772
  40.4 41.1 %collective-permute-start.6 = (f32[512,256]{1,0:T(8,128)S(1)}, f32[512,256]{1,0:T(8,128)S(1)}, u32[]{:S(2)}, u32[]{:S(2)}) collective-permute-start(f32[512,256]{1,0:T(8,128)S(1)} %get-tuple-element.19.away), channel_id=1, source_target_pairs={{1,2},{2,1},{3,4},{4,3},{5,6},{6,5},{7,8},{8,7},{9,10},{10,9},{11,... | collective-permute-start | bytes 1572872 | tf_op jit(solution)/shard_map/ppermute | solution.py:223
  44.0 37.4 %collective-permute-start.7 = (f32[512,256]{1,0:T(8,128)S(1)}, f32[512,256]{1,0:T(8,128)S(1)}, u32[]{:S(2)}, u32[]{:S(2)}) collective-permute-start(f32[512,256]{1,0:T(8,128)S(1)} %get-tuple-element.20.near), channel_id=1, source_target_pairs={{0,1},{1,0},{2,3},{3,2},{4,5},{5,4},{6,7},{7,6},{8,9},{9,8},{10,11... | collective-permute-start | bytes 1572872 | tf_op jit(solution)/shard_map/ppermute | solution.py:223
  46.5 3.4 %collective-permute-start.14 = (f32[256,256]{1,0:T(8,128)S(1)}, f32[256,256]{1,0:T(8,128)S(1)}, u32[]{:S(2)}, u32[]{:S(2)}) collective-permute-start(f32[256,256]{1,0:T(8,128)S(1)} %shard_map.33.mine), channel_id=1, source_target_pairs={{0,1},{1,0},{2,3},{3,2},{4,5},{5,4},{6,7},{7,6},{8,9},{9,8},{10,11... | collective-permute-start | bytes 786440 | tf_op jit(solution)/shard_map/ppermute | solution.py:223
  62.1 24.7 %collective-permute-start.18 = (f32[256,512]{1,0:T(8,128)S(1)}, f32[256,512]{1,0:T(8,128)S(1)}, u32[]{:S(2)}, u32[]{:S(2)}) collective-permute-start(f32[256,512]{1,0:T(8,128)S(1)} %get-tuple-element.26.b0), channel_id=1, source_target_pairs={{32,0},{33,1},{34,2},{35,3},{36,4},{37,5},{38,6},{39,7},{40,8},{41... | collective-permute-start | bytes 1572872 | tf_op jit(solution)/shard_map/ppermute | solution.py:223
  83.1 13.5 %collective-permute-start.15 = (f32[256,512]{1,0:T(8,128)S(1)}, f32[256,512]{1,0:T(8,128)S(1)}, u32[]{:S(2)}, u32[]{:S(2)}) collective-permute-start(f32[256,512]{1,0:T(8,128)S(1)} %get-tuple-element.23.b3), channel_id=1, source_target_pairs={{0,32},{1,33},{2,34},{3,35},{4,36},{5,37},{6,38},{7,39},{8,40},{9,... | collective-permute-start | bytes 1572872 | tf_op jit(solution)/shard_map/ppermute | solution.py:223

commit v5 on v4

--- a/solution.py
+++ b/solution.py
@@ -225,11 +225,25 @@
 
 HOLDERS = [(0, 0), (4, 0), (2, 1), (6, 1)]
 STEPS = [(0, 1), (1, 0), (7, 0)]
-ROWS_1 = [over_rows([(0, 0)], [target]) for target in HOLDERS[1:]]
-ROWS_2 = [over_rows(HOLDERS, [((z + step) % 8, h ^ flip) for z, h in HOLDERS]) for step, flip in STEPS]
-EVEN = [(0, 0), (4, 0), (2, 0), (6, 0)]
-COLS_1 = [over_columns([(0, 0)], [target]) for target in EVEN[1:]]
-COLS_2 = [over_columns(EVEN, [((y + step) % 8, flip) for y, _ in EVEN]) for step, flip in ((1, 0), (0, 1), (1, 1))]
+FIRST = [(0, 0), (2, 0), (6, 0), (4, 1)]
+ROWS_1 = [over_rows([(0, 0)], [target]) for target in FIRST[1:]]
+ROWS_2 = [
+    over_rows(FIRST, targets)
+    for targets in (
+        [(0, 1), (2, 1), (6, 1), (4, 0)],
+        [(1, 0), (3, 0), (5, 0), (3, 1)],
+        [(7, 0), (1, 1), (7, 1), (5, 1)],
+    )
+]
+COLS_1 = [over_columns([(0, 0)], [target]) for target in HOLDERS[1:]]
+COLS_2 = [
+    over_columns(HOLDERS, targets)
+    for targets in (
+        [(1, 0), (3, 0), (1, 1), (5, 1)],
+        [(7, 0), (5, 0), (3, 1), (7, 1)],
+        [(2, 0), (6, 0), (0, 1), (4, 1)],
+    )
+]
 CORES = [(device(r, c), device(r, c ^ 1)) for r in range(16) for c in range(32)]
 CHIPS = [
     (device(r, c), device(r, d)) for r in range(16) for c in range(32) for d in [c - 1 + 2 * (c % 2)] if 0 <= d < 32

time: 98.6 us -> 98.4 us (level)
  the two profiles are of different devices: /device:TPU:194 before, /device:TPU:130 now
where the time goes in v5:
time: 98.4 us; the launch traced here: 97.9 us
  waiting for transfers between devices  47.8 us (49%)
  starting transfers between devices  34 us (35%)
  Pallas kernels  14.7 us (15%)
  local copies, waits for them, and re-layouts  1.13 us (1%)
    ppermute x19, waiting for transfers between devices, send(): return lax.ppermute(x, AXES, pairs)  47.8 us
    ppermute x19, starting transfers between devices, send(): return lax.ppermute(x, AXES, pairs)  34 us
    pallas_call x1, Pallas kernels, body(): call(first_columns_kernel, (half, half, bf16(SPAN, SPAN), bf16(SPAN, SPAN...  3.71 us
    pallas_call x1, Pallas kernels, body(): call(rotations_kernel, (bf16(2, SPAN, SPAN),) * 2, [VMEM] * 2, (VMEM,) *...  3.28 us
  transfers between devices with their start and end apart: 19, of which 5 were waited for; matrix products, arithmetic and copies ran while one was open for 0% of the time, Pallas kernels for 14%

profile of v5, /device:TPU:130, one launch (start us, length us, event | category | flops | bytes accessed | tf_op | source)
XLA Modules:
  0.0 97.9 jit_solution(7876370670099141977)
XLA Ops:
  0.0 0.0 copy-start
  0.0 1.1 %constant_dynamic-slice_fusion.first.upper = f32[256,256]{1,0:T(8,128)S(1)} fusion(f32[1024,512]{1,0:T(8,128)} %matrix.3, s32[]{:T(128)S(6)} %select_n.11), kind=kLoop, calls=%fused_computation | loop fusion | bytes 524292 | tf_op jit(solution)/shard_map/dynamic_slice | solution.py:257
  1.1 0.7 collective-permute-start
  1.8 0.7 collective-permute-start.1
  2.5 0.7 collective-permute-start.2
  3.2 1.3 %collective-permute-start.10 = (f32[256,256]{1,0:T(8,128)S(1)}, f32[256,256]{1,0:T(8,128)S(1)}, u32[]{:S(2)}, u32[]{:S(2)}) collective-permute-start(f32[256,256]{1,0:T(8,128)S(1)} %shard_map.31.first), channel_id=1, source_target_pairs={{0,26},{1,27},{34,56},{35,57},{68,94},{69,95},{102,124},{103,125},... | collective-permute-start | bytes 786440 | tf_op jit(solution)/shard_map/ppermute | solution.py:223
  4.5 0.7 collective-permute-start.8
  5.2 0.0 collective-permute-done.t0
  5.2 0.7 collective-permute-start.9
  5.9 0.0 collective-permute-done.1.t1
  5.9 0.0 collective-permute-done.2.t2
  5.9 0.1 shard_map.28.t0
  6.0 1.3 %collective-permute-start.3 = (f32[256,256]{1,0:T(8,128)S(1)}, f32[256,256]{1,0:T(8,128)S(1)}, u32[]{:S(2)}, u32[]{:S(2)}) collective-permute-start(f32[256,256]{1,0:T(8,128)S(1)} %shard_map.28.t0), channel_id=1, source_target_pairs={{0,32},{128,160},{384,416},{288,256},{1,33},{129,161},{385,417},{2... | collective-permute-start | bytes 786440 | tf_op jit(solution)/shard_map/ppermute | solution.py:223
  7.3 0.7 collective-permute-start.4
  8.0 16.1 %collective-permute-done.10.t2 = f32[256,256]{1,0:T(8,128)S(1)} collective-permute-done((f32[256,256]{1,0:T(8,128)S(1)}, f32[256,256]{1,0:T(8,128)S(1)}, u32[]{:S(2)}, u32[]{:S(2)}) %collective-permute-start.10) | collective-permute-done | bytes 262176 | tf_op jit(solution)/shard_map/ppermute | solution.py:223
  24.1 0.7 collective-permute-start.5
  24.8 0.0 collective-permute-done.8.t0
  24.8 0.0 collective-permute-done.9.t1
  24.8 0.1 shard_map.32.first
  24.8 1.3 %collective-permute-start.11 = (f32[256,256]{1,0:T(8,128)S(1)}, f32[256,256]{1,0:T(8,128)S(1)}, u32[]{:S(2)}, u32[]{:S(2)}) collective-permute-start(f32[256,256]{1,0:T(8,128)S(1)} %shard_map.32.first), channel_id=1, source_target_pairs={{0,4},{16,12},{10,6},{26,22},{1,5},{17,13},{11,7},{27,23},{34,38},... | collective-permute-start | bytes 786440 | tf_op jit(solution)/shard_map/ppermute | solution.py:223
  26.1 1.3 %collective-permute-start.12 = (f32[256,256]{1,0:T(8,128)S(1)}, f32[256,256]{1,0:T(8,128)S(1)}, u32[]{:S(2)}, u32[]{:S(2)}) collective-permute-start(f32[256,256]{1,0:T(8,128)S(1)} %shard_map.32.first), channel_id=1, source_target_pairs={{0,28},{16,20},{10,14},{26,30},{1,29},{17,21},{11,15},{27,31},{34,... | collective-permute-start | bytes 786440 | tf_op jit(solution)/shard_map/ppermute | solution.py:223
  27.5 0.0 collective-permute-done.3.t1
  27.5 8.4 %collective-permute-start.13 = (f32[256,256]{1,0:T(8,128)S(1)}, f32[256,256]{1,0:T(8,128)S(1)}, u32[]{:S(2)}, u32[]{:S(2)}) collective-permute-start(f32[256,256]{1,0:T(8,128)S(1)} %shard_map.32.first), channel_id=1, source_target_pairs={{0,8},{16,24},{10,2},{26,18},{1,9},{17,25},{11,3},{27,19},{34,42},... | collective-permute-start | bytes 786440 | tf_op jit(solution)/shard_map/ppermute | solution.py:223
  35.9 0.0 collective-permute-done.4.t2
  35.9 0.0 collective-permute-done.5.t3
  35.9 0.0 copy-done
  35.9 3.7 %shard_map.29 = (f32[512,256]{1,0:T(8,128)S(1)}, f32[512,256]{1,0:T(8,128)S(1)}, bf16[512,512]{1,0:T(8,128)(2,1)S(1)}, bf16[512,512]{1,0:T(8,128)(2,1)S(1)}) custom-call(f32[1024,512]{1,0:T(8,128)S(1)} %copy-done, f32[256,256]{1,0:T(8,128)S(1)} %shard_map.28.t0, f32[256,256]{1,0:T(8,128)S(1)} %collective-permute-done.3.t1, ...), custom_call_target="tpu_custom_call" | custom-call | tf_op jit(solution)/shard_map/pallas_call | solution.py:270
  39.6 1.9 %collective-permute-start.16 = (f32[512,256]{1,0:T(8,128)S(1)}, f32[512,256]{1,0:T(8,128)S(1)}, u32[]{:S(2)}, u32[]{:S(2)}) collective-permute-start(f32[512,256]{1,0:T(8,128)S(1)} %get-tuple-element.24.away), channel_id=1, source_target_pairs={{1,2},{2,1},{3,4},{4,3},{5,6},{6,5},{7,8},{8,7},{9,10},{10,9},{11,... | collective-permute-start | bytes 1572872 | tf_op jit(solution)/shard_map/ppermute | solution.py:223
  41.6 1.9 %collective-permute-start.17 = (f32[512,256]{1,0:T(8,128)S(1)}, f32[512,256]{1,0:T(8,128)S(1)}, u32[]{:S(2)}, u32[]{:S(2)}) collective-permute-start(f32[512,256]{1,0:T(8,128)S(1)} %get-tuple-element.25.near), channel_id=1, source_target_pairs={{0,1},{1,0},{2,3},{3,2},{4,5},{5,4},{6,7},{7,6},{8,9},{9,8},{10,11... | collective-permute-start | bytes 1572872 | tf_op jit(solution)/shard_map/ppermute | solution.py:223
  43.5 0.0 copy-start.1
  43.5 1.1 %shard_map.30 = (f32[512,256]{1,0:T(8,128)S(1)}, f32[512,256]{1,0:T(8,128)S(1)}) custom-call(f32[1024,512]{1,0:T(8,128)S(1)} %copy-done, bf16[512,512]{1,0:T(8,128)(2,1)S(1)} %get-tuple-element.17.high, bf16[512,512]{1,0:T(8,128)(2,1)S(1)} %get-tuple-element.18.low), custom_call_target="tpu_custom_call" | custom-call | tf_op jit(solution)/shard_map/pallas_call | solution.py:279
  44.6 0.0 collective-permute-done.11.t0
  44.6 3.6 %collective-permute-start.6 = (f32[512,256]{1,0:T(8,128)S(1)}, f32[512,256]{1,0:T(8,128)S(1)}, u32[]{:S(2)}, u32[]{:S(2)}) collective-permute-start(f32[512,256]{1,0:T(8,128)S(1)} %get-tuple-element.19.away), channel_id=1, source_target_pairs={{1,2},{2,1},{3,4},{4,3},{5,6},{6,5},{7,8},{8,7},{9,10},{10,9},{11,... | collective-permute-start | bytes 1572872 | tf_op jit(solution)/shard_map/ppermute | solution.py:223
  48.2 0.0 collective-permute-done.12.t1
  48.2 1.9 %collective-permute-start.7 = (f32[512,256]{1,0:T(8,128)S(1)}, f32[512,256]{1,0:T(8,128)S(1)}, u32[]{:S(2)}, u32[]{:S(2)}) collective-permute-start(f32[512,256]{1,0:T(8,128)S(1)} %get-tuple-element.20.near), channel_id=1, source_target_pairs={{0,1},{1,0},{2,3},{3,2},{4,5},{5,4},{6,7},{7,6},{8,9},{9,8},{10,11... | collective-permute-start | bytes 1572872 | tf_op jit(solution)/shard_map/ppermute | solution.py:223
  50.2 0.0 collective-permute-done.13.t2
  50.2 0.1 shard_map.33.mine
  50.2 2.4 %collective-permute-start.14 = (f32[256,256]{1,0:T(8,128)S(1)}, f32[256,256]{1,0:T(8,128)S(1)}, u32[]{:S(2)}, u32[]{:S(2)}) collective-permute-start(f32[256,256]{1,0:T(8,128)S(1)} %shard_map.33.mine), channel_id=1, source_target_pairs={{0,1},{1,0},{2,3},{3,2},{4,5},{5,4},{6,7},{7,6},{8,9},{9,8},{10,11... | collective-permute-start | bytes 786440 | tf_op jit(solution)/shard_map/ppermute | solution.py:223
  52.7 1.1 %collective-permute-done.14.other = f32[256,256]{1,0:T(8,128)S(1)} collective-permute-done((f32[256,256]{1,0:T(8,128)S(1)}, f32[256,256]{1,0:T(8,128)S(1)}, u32[]{:S(2)}, u32[]{:S(2)}) %collective-permute-start.14) | collective-permute-done | bytes 262176 | tf_op jit(solution)/shard_map/ppermute | solution.py:223
  53.8 3.3 %shard_map.34 = (bf16[2,512,512]{2,1,0:T(8,128)(2,1)S(1)}, bf16[2,512,512]{2,1,0:T(8,128)(2,1)S(1)}) custom-call(f32[256,256]{1,0:T(8,128)S(1)} %shard_map.33.mine, f32[256,256]{1,0:T(8,128)S(1)} %collective-permute-done.14.other), custom_call_target="tpu_custom_call" | custom-call | tf_op jit(solution)/shard_map/pallas_call | solution.py:282
  57.1 3.6 %collective-permute-done.16.from_chip = f32[512,256]{1,0:T(8,128)S(1)} collective-permute-done((f32[512,256]{1,0:T(8,128)S(1)}, f32[512,256]{1,0:T(8,128)S(1)}, u32[]{:S(2)}, u32[]{:S(2)}) %collective-permute-start.16) | collective-permute-done | bytes 524320 | tf_op jit(solution)/shard_map/ppermute | solution.py:223
  60.7 0.0 collective-permute-done.17.from_core
  60.7 0.0 copy-done.1
  60.7 1.7 %shard_map.36 = (f32[256,512]{1,0:T(8,128)S(1)}, f32[256,512]{1,0:T(8,128)S(1)}) custom-call(s32[1,64]{1,0:T(1,128)S(1)} %copy-done.1, f32[512,256]{1,0:T(8,128)S(1)} %get-tuple-element.24.away, f32[512,256]{1,0:T(8,128)S(1)} %get-tuple-element.25.near, f32[512,256]{1,0:T(8,128)S(1)} %collective-permute-done.16.from_chip, ...), custom_call_target="tpu_custom_call" | custom-call | tf_op jit(solution)/shard_map/pallas_call | solution.py:295
  62.4 1.9 %collective-permute-start.18 = (f32[256,512]{1,0:T(8,128)S(1)}, f32[256,512]{1,0:T(8,128)S(1)}, u32[]{:S(2)}, u32[]{:S(2)}) collective-permute-start(f32[256,512]{1,0:T(8,128)S(1)} %get-tuple-element.26.b0), channel_id=1, source_target_pairs={{32,0},{33,1},{34,2},{35,3},{36,4},{37,5},{38,6},{39,7},{40,8},{41... | collective-permute-start | bytes 1572872 | tf_op jit(solution)/shard_map/ppermute | solution.py:223
  64.3 17.0 %collective-permute-done.6.from_chip = f32[512,256]{1,0:T(8,128)S(1)} collective-permute-done((f32[512,256]{1,0:T(8,128)S(1)}, f32[512,256]{1,0:T(8,128)S(1)}, u32[]{:S(2)}, u32[]{:S(2)}) %collective-permute-start.6) | collective-permute-done | bytes 524320 | tf_op jit(solution)/shard_map/ppermute | solution.py:223
  81.4 0.0 collective-permute-done.7.from_core
  81.4 1.7 %shard_map.35 = (f32[256,512]{1,0:T(8,128)S(1)}, f32[256,512]{1,0:T(8,128)S(1)}) custom-call(s32[1,64]{1,0:T(1,128)S(1)} %copy-done.1, f32[512,256]{1,0:T(8,128)S(1)} %get-tuple-element.19.away, f32[512,256]{1,0:T(8,128)S(1)} %get-tuple-element.20.near, f32[512,256]{1,0:T(8,128)S(1)} %collective-permute-done.6.from_chip, ...), custom_call_target="tpu_custom_call" | custom-call | tf_op jit(solution)/shard_map/pallas_call | solution.py:297
  83.0 1.9 %collective-permute-start.15 = (f32[256,512]{1,0:T(8,128)S(1)}, f32[256,512]{1,0:T(8,128)S(1)}, u32[]{:S(2)}, u32[]{:S(2)}) collective-permute-start(f32[256,512]{1,0:T(8,128)S(1)} %get-tuple-element.23.b3), channel_id=1, source_target_pairs={{0,32},{1,33},{2,34},{3,35},{4,36},{5,37},{6,38},{7,39},{8,40},{9,... | collective-permute-start | bytes 1572872 | tf_op jit(solution)/shard_map/ppermute | solution.py:223
  85.0 1.7 %shard_map.37.partial = f32[1024,512]{1,0:T(8,128)} custom-call(s32[1,64]{1,0:T(1,128)S(1)} %copy-done.1, f32[256,512]{1,0:T(8,128)S(1)} %get-tuple-element.26.b0, f32[256,512]{1,0:T(8,128)S(1)} %get-tuple-element.27.b1, f32[256,512]{1,0:T(8,128)S(1)} %get-tuple-element.28.b2, f32[256,512]{1,0:T(8,128)S(1)} %get-tuple-element.23.b3), custom_call_target="tpu_custom_call" | custom-call | tf_op jit(solution)/shard_map/pallas_call | solution.py:299
  86.7 0.0 collective-permute-done.18.below
  86.7 9.8 %collective-permute-done.15.above = f32[256,512]{1,0:T(8,128)S(1)} collective-permute-done((f32[256,512]{1,0:T(8,128)S(1)}, f32[256,512]{1,0:T(8,128)S(1)}, u32[]{:S(2)}, u32[]{:S(2)}) %collective-permute-start.15) | collective-permute-done | bytes 524320 | tf_op jit(solution)/shard_map/ppermute | solution.py:223
  96.5 1.4 %shard_map.38 = f32[1024,512]{1,0:T(8,128)} custom-call(s32[1,64]{1,0:T(1,128)S(1)} %copy-done.1, f32[256,512]{1,0:T(8,128)S(1)} %collective-permute-done.15.above, f32[256,512]{1,0:T(8,128)S(1)} %collective-permute-done.18.below, f32[1024,512]{1,0:T(8,128)} %shard_map.37.partial), custom_call_target="tpu_custom_call", output_to_operand_aliasing={{}: (3, {})} | custom-call | tf_op jit(solution)/shard_map/pallas_call | solution.py:302
  (1 shorter events, 0.0 us)
Async XLA Ops:
  0.0 35.9 %copy-start = (f32[1024,512]{1,0:T(8,128)S(1)}, f32[1024,512]{1,0:T(8,128)}, u32[]{:S(2)}) copy-start(f32[1024,512]{1,0:T(8,128)} %matrix.3) | copy-start | bytes 6291460
  1.1 4.1 %collective-permute-start = (f32[256,256]{1,0:T(8,128)S(1)}, f32[256,256]{1,0:T(8,128)S(1)}, u32[]{:S(2)}, u32[]{:S(2)}) collective-permute-start(f32[256,256]{1,0:T(8,128)S(1)} %constant_dynamic-slice_fusion.first.upper), channel_id=1, source_target_pairs={{0,128},{1,129},{34,162},{35,163},{68,196},{69,197},{102,230},{103... | collective-permute-start | bytes 786440 | tf_op jit(solution)/shard_map/ppermute | solution.py:223
  1.8 4.1 %collective-permute-start.1 = (f32[256,256]{1,0:T(8,128)S(1)}, f32[256,256]{1,0:T(8,128)S(1)}, u32[]{:S(2)}, u32[]{:S(2)}) collective-permute-start(f32[256,256]{1,0:T(8,128)S(1)} %constant_dynamic-slice_fusion.first.upper), channel_id=1, source_target_pairs={{0,384},{1,385},{34,418},{35,419},{68,452},{69,453},{102,486},{103... | collective-permute-start | bytes 786440 | tf_op jit(solution)/shard_map/ppermute | solution.py:223
  2.5 3.4 %collective-permute-start.2 = (f32[256,256]{1,0:T(8,128)S(1)}, f32[256,256]{1,0:T(8,128)S(1)}, u32[]{:S(2)}, u32[]{:S(2)}) collective-permute-start(f32[256,256]{1,0:T(8,128)S(1)} %constant_dynamic-slice_fusion.first.upper), channel_id=1, source_target_pairs={{0,288},{1,289},{34,258},{35,259},{68,356},{69,357},{102,326},{103... | collective-permute-start | bytes 786440 | tf_op jit(solution)/shard_map/ppermute | solution.py:223
  3.2 20.9 %collective-permute-start.10 = (f32[256,256]{1,0:T(8,128)S(1)}, f32[256,256]{1,0:T(8,128)S(1)}, u32[]{:S(2)}, u32[]{:S(2)}) collective-permute-start(f32[256,256]{1,0:T(8,128)S(1)} %shard_map.31.first), channel_id=1, source_target_pairs={{0,26},{1,27},{34,56},{35,57},{68,94},{69,95},{102,124},{103,125},... | collective-permute-start | bytes 786440 | tf_op jit(solution)/shard_map/ppermute | solution.py:223
  4.5 20.3 %collective-permute-start.8 = (f32[256,256]{1,0:T(8,128)S(1)}, f32[256,256]{1,0:T(8,128)S(1)}, u32[]{:S(2)}, u32[]{:S(2)}) collective-permute-start(f32[256,256]{1,0:T(8,128)S(1)} %shard_map.31.first), channel_id=1, source_target_pairs={{0,16},{1,17},{34,50},{35,51},{68,84},{69,85},{102,118},{103,119},... | collective-permute-start | bytes 786440 | tf_op jit(solution)/shard_map/ppermute | solution.py:223
  5.2 19.6 %collective-permute-start.9 = (f32[256,256]{1,0:T(8,128)S(1)}, f32[256,256]{1,0:T(8,128)S(1)}, u32[]{:S(2)}, u32[]{:S(2)}) collective-permute-start(f32[256,256]{1,0:T(8,128)S(1)} %shard_map.31.first), channel_id=1, source_target_pairs={{0,10},{1,11},{34,40},{35,41},{68,78},{69,79},{102,108},{103,109},... | collective-permute-start | bytes 786440 | tf_op jit(solution)/shard_map/ppermute | solution.py:223
  6.0 21.5 %collective-permute-start.3 = (f32[256,256]{1,0:T(8,128)S(1)}, f32[256,256]{1,0:T(8,128)S(1)}, u32[]{:S(2)}, u32[]{:S(2)}) collective-permute-start(f32[256,256]{1,0:T(8,128)S(1)} %shard_map.28.t0), channel_id=1, source_target_pairs={{0,32},{128,160},{384,416},{288,256},{1,33},{129,161},{385,417},{2... | collective-permute-start | bytes 786440 | tf_op jit(solution)/shard_map/ppermute | solution.py:223
  7.3 28.6 %collective-permute-start.4 = (f32[256,256]{1,0:T(8,128)S(1)}, f32[256,256]{1,0:T(8,128)S(1)}, u32[]{:S(2)}, u32[]{:S(2)}) collective-permute-start(f32[256,256]{1,0:T(8,128)S(1)} %shard_map.28.t0), channel_id=1, source_target_pairs={{0,64},{128,192},{384,320},{288,224},{1,65},{129,193},{385,321},{2... | collective-permute-start | bytes 786440 | tf_op jit(solution)/shard_map/ppermute | solution.py:223
  24.1 11.8 %collective-permute-start.5 = (f32[256,256]{1,0:T(8,128)S(1)}, f32[256,256]{1,0:T(8,128)S(1)}, u32[]{:S(2)}, u32[]{:S(2)}) collective-permute-start(f32[256,256]{1,0:T(8,128)S(1)} %shard_map.28.t0), channel_id=1, source_target_pairs={{0,448},{128,96},{384,480},{288,352},{1,449},{129,97},{385,481},{2... | collective-permute-start | bytes 786440 | tf_op jit(solution)/shard_map/ppermute | solution.py:223
  24.8 19.7 %collective-permute-start.11 = (f32[256,256]{1,0:T(8,128)S(1)}, f32[256,256]{1,0:T(8,128)S(1)}, u32[]{:S(2)}, u32[]{:S(2)}) collective-permute-start(f32[256,256]{1,0:T(8,128)S(1)} %shard_map.32.first), channel_id=1, source_target_pairs={{0,4},{16,12},{10,6},{26,22},{1,5},{17,13},{11,7},{27,23},{34,38},... | collective-permute-start | bytes 786440 | tf_op jit(solution)/shard_map/ppermute | solution.py:223
  26.1 22.1 %collective-permute-start.12 = (f32[256,256]{1,0:T(8,128)S(1)}, f32[256,256]{1,0:T(8,128)S(1)}, u32[]{:S(2)}, u32[]{:S(2)}) collective-permute-start(f32[256,256]{1,0:T(8,128)S(1)} %shard_map.32.first), channel_id=1, source_target_pairs={{0,28},{16,20},{10,14},{26,30},{1,29},{17,21},{11,15},{27,31},{34,... | collective-permute-start | bytes 786440 | tf_op jit(solution)/shard_map/ppermute | solution.py:223
  27.5 22.7 %collective-permute-start.13 = (f32[256,256]{1,0:T(8,128)S(1)}, f32[256,256]{1,0:T(8,128)S(1)}, u32[]{:S(2)}, u32[]{:S(2)}) collective-permute-start(f32[256,256]{1,0:T(8,128)S(1)} %shard_map.32.first), channel_id=1, source_target_pairs={{0,8},{16,24},{10,2},{26,18},{1,9},{17,25},{11,3},{27,19},{34,42},... | collective-permute-start | bytes 786440 | tf_op jit(solution)/shard_map/ppermute | solution.py:223
  39.6 21.1 %collective-permute-start.16 = (f32[512,256]{1,0:T(8,128)S(1)}, f32[512,256]{1,0:T(8,128)S(1)}, u32[]{:S(2)}, u32[]{:S(2)}) collective-permute-start(f32[512,256]{1,0:T(8,128)S(1)} %get-tuple-element.24.away), channel_id=1, source_target_pairs={{1,2},{2,1},{3,4},{4,3},{5,6},{6,5},{7,8},{8,7},{9,10},{10,9},{11,... | collective-permute-start | bytes 1572872 | tf_op jit(solution)/shard_map/ppermute | solution.py:223
  41.6 19.1 %collective-permute-start.17 = (f32[512,256]{1,0:T(8,128)S(1)}, f32[512,256]{1,0:T(8,128)S(1)}, u32[]{:S(2)}, u32[]{:S(2)}) collective-permute-start(f32[512,256]{1,0:T(8,128)S(1)} %get-tuple-element.25.near), channel_id=1, source_target_pairs={{0,1},{1,0},{2,3},{3,2},{4,5},{5,4},{6,7},{7,6},{8,9},{9,8},{10,11... | collective-permute-start | bytes 1572872 | tf_op jit(solution)/shard_map/ppermute | solution.py:223
  43.5 17.2 %copy-start.1 = (s32[1,64]{1,0:T(1,128)S(1)}, s32[1,64]{1,0:T(1,128)}, u32[]{:S(2)}) copy-start(s32[1,64]{1,0:T(1,128)} %moves.7) | copy-start | bytes 772
  44.6 36.8 %collective-permute-start.6 = (f32[512,256]{1,0:T(8,128)S(1)}, f32[512,256]{1,0:T(8,128)S(1)}, u32[]{:S(2)}, u32[]{:S(2)}) collective-permute-start(f32[512,256]{1,0:T(8,128)S(1)} %get-tuple-element.19.away), channel_id=1, source_target_pairs={{1,2},{2,1},{3,4},{4,3},{5,6},{6,5},{7,8},{8,7},{9,10},{10,9},{11,... | collective-permute-start | bytes 1572872 | tf_op jit(solution)/shard_map/ppermute | solution.py:223
  48.2 33.1 %collective-permute-start.7 = (f32[512,256]{1,0:T(8,128)S(1)}, f32[512,256]{1,0:T(8,128)S(1)}, u32[]{:S(2)}, u32[]{:S(2)}) collective-permute-start(f32[512,256]{1,0:T(8,128)S(1)} %get-tuple-element.20.near), channel_id=1, source_target_pairs={{0,1},{1,0},{2,3},{3,2},{4,5},{5,4},{6,7},{7,6},{8,9},{9,8},{10,11... | collective-permute-start | bytes 1572872 | tf_op jit(solution)/shard_map/ppermute | solution.py:223
  50.2 3.6 %collective-permute-start.14 = (f32[256,256]{1,0:T(8,128)S(1)}, f32[256,256]{1,0:T(8,128)S(1)}, u32[]{:S(2)}, u32[]{:S(2)}) collective-permute-start(f32[256,256]{1,0:T(8,128)S(1)} %shard_map.33.mine), channel_id=1, source_target_pairs={{0,1},{1,0},{2,3},{3,2},{4,5},{5,4},{6,7},{7,6},{8,9},{9,8},{10,11... | collective-permute-start | bytes 786440 | tf_op jit(solution)/shard_map/ppermute | solution.py:223
  62.4 24.3 %collective-permute-start.18 = (f32[256,512]{1,0:T(8,128)S(1)}, f32[256,512]{1,0:T(8,128)S(1)}, u32[]{:S(2)}, u32[]{:S(2)}) collective-permute-start(f32[256,512]{1,0:T(8,128)S(1)} %get-tuple-element.26.b0), channel_id=1, source_target_pairs={{32,0},{33,1},{34,2},{35,3},{36,4},{37,5},{38,6},{39,7},{40,8},{41... | collective-permute-start | bytes 1572872 | tf_op jit(solution)/shard_map/ppermute | solution.py:223
  83.0 13.5 %collective-permute-start.15 = (f32[256,512]{1,0:T(8,128)S(1)}, f32[256,512]{1,0:T(8,128)S(1)}, u32[]{:S(2)}, u32[]{:S(2)}) collective-permute-start(f32[256,512]{1,0:T(8,128)S(1)} %get-tuple-element.23.b3), channel_id=1, source_target_pairs={{0,32},{1,33},{2,34},{3,35},{4,36},{5,37},{6,38},{7,39},{8,40},{9,... | collective-permute-start | bytes 1572872 | tf_op jit(solution)/shard_map/ppermute | solution.py:223
